TPU v7x, 128 devices: a whole 4x4x4 slice. The times are simulated.
128 devices in a mesh: leaf: 64 (over y, z, x), sub: 2 (over core).
Axes of the slice: x: 4, y: 4, z: 4, core: 2. Of those that a mesh axis runs over, the one named last changes fastest.
Arguments:
- multipole: bfloat16 [32768, 256], P(('leaf', 'sub')), may hold values from -6 to 6
- positions: float32 [32768, 3, 128], P(('leaf', 'sub')), may hold values from 0 to 1
- charges: float32 [32768, 128], P(('leaf', 'sub')), may hold values from -0.06 to 0.06
- translate_ops: bfloat16 [64, 256, 256], replicated, may hold values from -0.02734375 to 0.02734375
- upward_ops: bfloat16 [8, 256, 256], replicated, may hold values from -0.015625 to 0.015625
- downward_ops: bfloat16 [8, 256, 256], replicated, may hold values from -0.375 to 0.375
- top_weight: float32 [64, 64], replicated, may hold values from -0.75 to 0.75
- send_cells: int32 [16384, 16], P(('leaf', 'sub')), may hold values from 0 to 255
- send_leaves: int32 [16384, 4], P(('leaf', 'sub')), may hold values from 0 to 255
- list_source: int32 [32768, 189], P(('leaf', 'sub')), may hold values from 0 to 2303, as said below
- list_operator: int32 [32768, 189], P(('leaf', 'sub')), may hold values from 0 to 63
- near_leaves: int32 [32768, 27], P(('leaf', 'sub')), may hold values from 0 to 767, as said below
- move_counts: int32 [128, 2], P(('leaf', 'sub')), may hold values from 0 to 8, as said below
Outputs:
- local_exp: float32 [32768, 256], P(('leaf', 'sub'))
- potential: float32 [32768, 128], P(('leaf', 'sub'))
- arrivals: float32 [2048, 5, 128], P(('leaf', 'sub'))
Inputs may be any that keep to these rules, and one draw needn't show every extreme that they name: `list_source`: an entry below 256 is a leaf of the same rank; an entry 256 + e * 16 + s is slot s of the multipoles rank e sends to it. `near_leaves`: an entry below 256 is a leaf of the same rank; an entry 256 + e * 4 + s is slot s of the particle blocks rank e sends to it. move_counts[0, 0] and move_counts[127, 1] are 0, every other entry is 1 or more; each column reaches 8 at some rank.
All inputs are finite; a program needn't handle non-finite values.
Results may differ from a plain program's by a relative error of at most 0.0029.
Values may be sent and summed in bfloat16 or wider, within the bound.
A program may use at most 64 MiB of HBM per device.

v0:
```python
import math

import jax
import jax.numpy as jnp
from jax import lax
from jax.sharding import PartitionSpec as P

MCAP = 8
TOP = 64


SOFTENING = 0.01


def shifted(x, axis, by):
    devices = lax.axis_size(axis)
    pairs = [(i, i + by) for i in range(devices) if 0 <= i + by < devices]
    return lax.ppermute(x, axis, pairs)


def stacked_octants(row_data, first_cell):
    row_count = row_data.shape[0]
    octant = (first_cell + jnp.arange(row_count, dtype=jnp.int32)) % 8
    octant_mask = (octant[:, None] == jnp.arange(8, dtype=jnp.int32)[None, :]).astype(
        row_data.dtype
    )
    return (octant_mask[:, :, None] * row_data[:, None, :]).reshape(
        row_count, 8 * row_data.shape[1]
    )


def per_device(
    multipole,
    positions,
    charges,
    translate_ops,
    upward_ops,
    downward_ops,
    top_weight,
    send_cells,
    send_leaves,
    list_source,
    list_operator,
    near_leaves,
    move_counts,
):
    highest = lax.Precision.HIGHEST
    cell_count = multipole.shape[0]
    coef_width = multipole.shape[1]
    leaf_size = positions.shape[2]
    rank_count = lax.axis_size(("leaf", "sub"))
    rank_index = lax.axis_index(("leaf", "sub"))
    all_cells = cell_count * rank_count
    first_cell = rank_index * cell_count
    out_cells = multipole[send_cells]
    out_pos = positions[send_leaves]
    out_charge = charges[send_leaves]
    got_cells = lax.all_to_all(out_cells, ("leaf", "sub"), split_axis=0, concat_axis=0, tiled=True)
    got_pos, got_charge = (
        lax.all_to_all(out_pos, ("leaf", "sub"), split_axis=0, concat_axis=0, tiled=True),
        lax.all_to_all(out_charge, ("leaf", "sub"), split_axis=0, concat_axis=0, tiled=True),
    )
    got_cells = got_cells.reshape(-1, coef_width)
    got_pos = got_pos.reshape(-1, 3, leaf_size)
    got_charge = got_charge.reshape(-1, leaf_size)
    upward = jnp.dot(
        stacked_octants(multipole, first_cell),
        upward_ops.reshape(-1, coef_width),
        preferred_element_type=jnp.float32,
    )
    cell_top = (first_cell + jnp.arange(cell_count, dtype=jnp.int32)) * TOP // all_cells
    member = (jnp.arange(TOP, dtype=jnp.int32)[:, None] == cell_top[None, :]).astype(jnp.float32)
    partial_value = jnp.dot(member, upward, precision=highest, preferred_element_type=jnp.float32)
    top_sums = lax.psum(partial_value, ("leaf", "sub"))
    coarse = jnp.dot(
        top_weight, top_sums, precision=highest, preferred_element_type=jnp.float32
    ).astype(jnp.bfloat16)
    cell_pick = (cell_top[:, None] == jnp.arange(TOP, dtype=jnp.int32)[None, :]).astype(
        jnp.bfloat16
    )
    coarse_cell = jnp.dot(cell_pick, coarse, preferred_element_type=jnp.float32).astype(
        jnp.bfloat16
    )
    far_top = jnp.dot(
        stacked_octants(coarse_cell, first_cell),
        downward_ops.reshape(-1, coef_width),
        preferred_element_type=jnp.float32,
    )
    source_table = jnp.concatenate([multipole, got_cells], 0)
    op_count = translate_ops.shape[0]
    list_width = list_source.shape[1]
    ops_flat = translate_ops.reshape(-1, coef_width)
    m2l_block = math.gcd(cell_count, 32)

    def translate_block(inputs):
        source_ids, operator_ids = inputs
        picked = source_table[source_ids]
        one_hot = (
            operator_ids[:, :, None] == jnp.arange(op_count, dtype=jnp.int32)[None, None, :]
        ).astype(jnp.bfloat16)
        grouped = jnp.einsum(
            "cjk,cjf->ckf", one_hot, picked, preferred_element_type=jnp.float32
        ).astype(jnp.bfloat16)
        return jnp.dot(
            grouped.reshape(source_ids.shape[0], -1), ops_flat, preferred_element_type=jnp.float32
        )

    translated = lax.map(
        translate_block,
        (
            list_source.reshape(-1, m2l_block, list_width),
            list_operator.reshape(-1, m2l_block, list_width),
        ),
    ).reshape(cell_count, coef_width)
    local_exp = translated + far_top
    pos_table = jnp.concatenate([positions, got_pos], 0)
    charge_table = jnp.concatenate([charges, got_charge], 0)
    block_size = math.gcd(cell_count, 16)
    near_count = near_leaves.shape[1]

    def one_block(inputs):
        target, near_list = inputs
        picked_pos = pos_table[near_list]
        picked_charge = charge_table[near_list]
        distance = jnp.zeros((target.shape[0], near_count, leaf_size, leaf_size), jnp.float32)
        for axis_id in range(3):
            offset = target[:, None, axis_id, :, None] - picked_pos[:, :, axis_id, None, :]
            distance = distance + offset * offset
        kernel = lax.rsqrt(distance + SOFTENING)
        return jnp.sum(kernel * picked_charge[:, :, None, :], axis=(1, 3))

    potential = lax.map(
        one_block,
        (
            positions.reshape(-1, block_size, 3, leaf_size),
            near_leaves.reshape(-1, block_size, near_count),
        ),
    ).reshape(cell_count, leaf_size)
    payload = jnp.concatenate([positions, charges[:, None, :], potential[:, None, :]], 1)
    slot_total = payload.shape[0]
    slot_index = jnp.arange(MCAP, dtype=jnp.int32)
    lower_usable = slot_index < move_counts[0, 0]
    lower_pack = jnp.where(lower_usable[:, None, None], payload[:MCAP], 0.0)
    upper_usable = slot_index < move_counts[0, 1]
    upper_pack = jnp.where(upper_usable[:, None, None], payload[slot_total - 1 - slot_index], 0.0)
    from_upper = shifted(lower_pack, ("leaf", "sub"), -1)
    from_lower = shifted(upper_pack, ("leaf", "sub"), 1)
    arrivals = jnp.concatenate([from_upper, from_lower], 0)
    return (local_exp, potential, arrivals)


def solution(mesh):
    placed = (
        P(("leaf", "sub"), None),
        P(("leaf", "sub"), None, None),
        P(("leaf", "sub"), None),
        P(),
        P(),
        P(),
        P(),
        P(("leaf", "sub"), None),
        P(("leaf", "sub"), None),
        P(("leaf", "sub"), None),
        P(("leaf", "sub"), None),
        P(("leaf", "sub"), None),
        P(("leaf", "sub"), None),
    )
    return jax.shard_map(
        per_device,
        mesh=mesh,
        in_specs=placed,
        out_specs=(
            P(("leaf", "sub"), None),
            P(("leaf", "sub"), None),
            P(("leaf", "sub"), None, None),
        ),
        check_vma=False,
    )
```

profile of v0, /device:TPU:8, one launch (start us, length us, event | category | flops | bytes accessed | tf_op | source)
XLA Modules:
  0.0 791.5 jit_solution(6169676454415698660)
XLA Ops:
  13.3 10.4 %all-to-all-start.2 = ((f32[128,4,128]{2,1,0:T(4,128)}), f32[128,4,128]{2,1,0:T(4,128)S(1)}, u32[]{:S(2)}, u32[]{:S(2)}) async-start(f32[128,4,128]{2,1,0:T(4,128)} %bitcast.25), calls=%async_computation.2 | async-start | bytes 524288 | tf_op jit(solution)/shard_map/all_to_all | solution.py:61
  27.9 6.0 all-to-all-done.2
  33.8 5.4 all-to-all-start.1
  45.6 9.0 %gather_fusion.3 = bf16[2048,256]{1,0:T(8,128)(2,1)} fusion(bf16[256,256]{1,0:T(8,128)(2,1)S(1)} %copy-done.1, s32[2048]{0:T(1024)S(1)} %broadcast_clamp_fusion), kind=kCustom, calls=%fused_computation.3 | custom fusion | bytes 2105344 | tf_op jit(solution)/shard_map/gather | solution.py:55
  55.3 100.1 %all-reduce.2.cloned.1.call-done = f32[64,256]{1,0:T(8,128)} async-done(((f32[64,256]{1,0:T(8,128)}), f32[64,256]{1,0:T(8,128)}) %all-reduce.2.cloned.1.call-update) | async-done | bytes 65552 | tf_op jit(solution)/shard_map/psum | solution.py:74
  156.6 6.6 all-to-all-start
  165.4 292.8 %while.21 = (s32[]{:T(128)}, f32[16,16,128]{2,1,0:T(8,128)}, f32[16,16,3,128]{3,1,0,2:T(8,128)S(1)}, s32[16,16,27]{2,1,0:T(8,128)}, f32[768,3,128]{2,1,0:T(4,128)}, /*index=5*/f32[768,128]{1,0:T(8,128)S(1)}, s32[]{:T(128)}) while((s32[]{:T(128)}, f32[16,16,128]{2,1,0:T(8,128)}, f32[16,16,3,128]{3,1,0,2:T(8,128)S(1)}, s32[16,16,27]{2,1,0:T(8,128)}, ...), condition=%wide.region_5.6_spmd, body=%wide.region_3.5_spmd.sunk | while | flops 77857040 | bytes 5914529 | solution.py:132
  170.7 12.3 %multiply_reduce_fusion.2 = f32[16,128]{1,0:T(8,128)S(1)} fusion(f32[16,27,128]{2,1,0:T(8,128)S(1)} %reshape.304, f32[16,27,128]{2,1,0:T(8,128)S(1)} %get-tuple-element.225, f32[16,128]{1,0:T(8,128)S(1)} %get-tuple-element.226, f32[16,27,128]{2,1,0:T(8,128)S(1)} %get-tuple-element.227, f32[16,128]{1,0:T(8,128)S(1)} %get-tuple-element.228, ...), kind=kLoop, calls=%fused_computation.16.clone.1 | loop fusion | flops 77854720 | bytes 917504 | tf_op jit(solution)/shard_map/while/body/eval_jaxpr/reduce_sum | solution.py:130
  189.0 12.3 %multiply_reduce_fusion.2 = f32[16,128]{1,0:T(8,128)S(1)} fusion(f32[16,27,128]{2,1,0:T(8,128)S(1)} %reshape.304, f32[16,27,128]{2,1,0:T(8,128)S(1)} %get-tuple-element.225, f32[16,128]{1,0:T(8,128)S(1)} %get-tuple-element.226, f32[16,27,128]{2,1,0:T(8,128)S(1)} %get-tuple-element.227, f32[16,128]{1,0:T(8,128)S(1)} %get-tuple-element.228, ...), kind=kLoop, calls=%fused_computation.16.clone.1 | loop fusion | flops 77854720 | bytes 917504 | tf_op jit(solution)/shard_map/while/body/eval_jaxpr/reduce_sum | solution.py:130
  207.3 12.3 %multiply_reduce_fusion.2 = f32[16,128]{1,0:T(8,128)S(1)} fusion(f32[16,27,128]{2,1,0:T(8,128)S(1)} %reshape.304, f32[16,27,128]{2,1,0:T(8,128)S(1)} %get-tuple-element.225, f32[16,128]{1,0:T(8,128)S(1)} %get-tuple-element.226, f32[16,27,128]{2,1,0:T(8,128)S(1)} %get-tuple-element.227, f32[16,128]{1,0:T(8,128)S(1)} %get-tuple-element.228, ...), kind=kLoop, calls=%fused_computation.16.clone.1 | loop fusion | flops 77854720 | bytes 917504 | tf_op jit(solution)/shard_map/while/body/eval_jaxpr/reduce_sum | solution.py:130
  225.6 12.3 %multiply_reduce_fusion.2 = f32[16,128]{1,0:T(8,128)S(1)} fusion(f32[16,27,128]{2,1,0:T(8,128)S(1)} %reshape.304, f32[16,27,128]{2,1,0:T(8,128)S(1)} %get-tuple-element.225, f32[16,128]{1,0:T(8,128)S(1)} %get-tuple-element.226, f32[16,27,128]{2,1,0:T(8,128)S(1)} %get-tuple-element.227, f32[16,128]{1,0:T(8,128)S(1)} %get-tuple-element.228, ...), kind=kLoop, calls=%fused_computation.16.clone.1 | loop fusion | flops 77854720 | bytes 917504 | tf_op jit(solution)/shard_map/while/body/eval_jaxpr/reduce_sum | solution.py:130
  243.9 12.3 %multiply_reduce_fusion.2 = f32[16,128]{1,0:T(8,128)S(1)} fusion(f32[16,27,128]{2,1,0:T(8,128)S(1)} %reshape.304, f32[16,27,128]{2,1,0:T(8,128)S(1)} %get-tuple-element.225, f32[16,128]{1,0:T(8,128)S(1)} %get-tuple-element.226, f32[16,27,128]{2,1,0:T(8,128)S(1)} %get-tuple-element.227, f32[16,128]{1,0:T(8,128)S(1)} %get-tuple-element.228, ...), kind=kLoop, calls=%fused_computation.16.clone.1 | loop fusion | flops 77854720 | bytes 917504 | tf_op jit(solution)/shard_map/while/body/eval_jaxpr/reduce_sum | solution.py:130
  262.2 12.3 %multiply_reduce_fusion.2 = f32[16,128]{1,0:T(8,128)S(1)} fusion(f32[16,27,128]{2,1,0:T(8,128)S(1)} %reshape.304, f32[16,27,128]{2,1,0:T(8,128)S(1)} %get-tuple-element.225, f32[16,128]{1,0:T(8,128)S(1)} %get-tuple-element.226, f32[16,27,128]{2,1,0:T(8,128)S(1)} %get-tuple-element.227, f32[16,128]{1,0:T(8,128)S(1)} %get-tuple-element.228, ...), kind=kLoop, calls=%fused_computation.16.clone.1 | loop fusion | flops 77854720 | bytes 917504 | tf_op jit(solution)/shard_map/while/body/eval_jaxpr/reduce_sum | solution.py:130
  280.5 12.3 %multiply_reduce_fusion.2 = f32[16,128]{1,0:T(8,128)S(1)} fusion(f32[16,27,128]{2,1,0:T(8,128)S(1)} %reshape.304, f32[16,27,128]{2,1,0:T(8,128)S(1)} %get-tuple-element.225, f32[16,128]{1,0:T(8,128)S(1)} %get-tuple-element.226, f32[16,27,128]{2,1,0:T(8,128)S(1)} %get-tuple-element.227, f32[16,128]{1,0:T(8,128)S(1)} %get-tuple-element.228, ...), kind=kLoop, calls=%fused_computation.16.clone.1 | loop fusion | flops 77854720 | bytes 917504 | tf_op jit(solution)/shard_map/while/body/eval_jaxpr/reduce_sum | solution.py:130
  298.8 12.3 %multiply_reduce_fusion.2 = f32[16,128]{1,0:T(8,128)S(1)} fusion(f32[16,27,128]{2,1,0:T(8,128)S(1)} %reshape.304, f32[16,27,128]{2,1,0:T(8,128)S(1)} %get-tuple-element.225, f32[16,128]{1,0:T(8,128)S(1)} %get-tuple-element.226, f32[16,27,128]{2,1,0:T(8,128)S(1)} %get-tuple-element.227, f32[16,128]{1,0:T(8,128)S(1)} %get-tuple-element.228, ...), kind=kLoop, calls=%fused_computation.16.clone.1 | loop fusion | flops 77854720 | bytes 917504 | tf_op jit(solution)/shard_map/while/body/eval_jaxpr/reduce_sum | solution.py:130
  317.1 12.3 %multiply_reduce_fusion.2 = f32[16,128]{1,0:T(8,128)S(1)} fusion(f32[16,27,128]{2,1,0:T(8,128)S(1)} %reshape.304, f32[16,27,128]{2,1,0:T(8,128)S(1)} %get-tuple-element.225, f32[16,128]{1,0:T(8,128)S(1)} %get-tuple-element.226, f32[16,27,128]{2,1,0:T(8,128)S(1)} %get-tuple-element.227, f32[16,128]{1,0:T(8,128)S(1)} %get-tuple-element.228, ...), kind=kLoop, calls=%fused_computation.16.clone.1 | loop fusion | flops 77854720 | bytes 917504 | tf_op jit(solution)/shard_map/while/body/eval_jaxpr/reduce_sum | solution.py:130
  335.4 12.3 %multiply_reduce_fusion.2 = f32[16,128]{1,0:T(8,128)S(1)} fusion(f32[16,27,128]{2,1,0:T(8,128)S(1)} %reshape.304, f32[16,27,128]{2,1,0:T(8,128)S(1)} %get-tuple-element.225, f32[16,128]{1,0:T(8,128)S(1)} %get-tuple-element.226, f32[16,27,128]{2,1,0:T(8,128)S(1)} %get-tuple-element.227, f32[16,128]{1,0:T(8,128)S(1)} %get-tuple-element.228, ...), kind=kLoop, calls=%fused_computation.16.clone.1 | loop fusion | flops 77854720 | bytes 917504 | tf_op jit(solution)/shard_map/while/body/eval_jaxpr/reduce_sum | solution.py:130
  353.7 12.3 %multiply_reduce_fusion.2 = f32[16,128]{1,0:T(8,128)S(1)} fusion(f32[16,27,128]{2,1,0:T(8,128)S(1)} %reshape.304, f32[16,27,128]{2,1,0:T(8,128)S(1)} %get-tuple-element.225, f32[16,128]{1,0:T(8,128)S(1)} %get-tuple-element.226, f32[16,27,128]{2,1,0:T(8,128)S(1)} %get-tuple-element.227, f32[16,128]{1,0:T(8,128)S(1)} %get-tuple-element.228, ...), kind=kLoop, calls=%fused_computation.16.clone.1 | loop fusion | flops 77854720 | bytes 917504 | tf_op jit(solution)/shard_map/while/body/eval_jaxpr/reduce_sum | solution.py:130
  372.0 12.3 %multiply_reduce_fusion.2 = f32[16,128]{1,0:T(8,128)S(1)} fusion(f32[16,27,128]{2,1,0:T(8,128)S(1)} %reshape.304, f32[16,27,128]{2,1,0:T(8,128)S(1)} %get-tuple-element.225, f32[16,128]{1,0:T(8,128)S(1)} %get-tuple-element.226, f32[16,27,128]{2,1,0:T(8,128)S(1)} %get-tuple-element.227, f32[16,128]{1,0:T(8,128)S(1)} %get-tuple-element.228, ...), kind=kLoop, calls=%fused_computation.16.clone.1 | loop fusion | flops 77854720 | bytes 917504 | tf_op jit(solution)/shard_map/while/body/eval_jaxpr/reduce_sum | solution.py:130
  390.3 12.3 %multiply_reduce_fusion.2 = f32[16,128]{1,0:T(8,128)S(1)} fusion(f32[16,27,128]{2,1,0:T(8,128)S(1)} %reshape.304, f32[16,27,128]{2,1,0:T(8,128)S(1)} %get-tuple-element.225, f32[16,128]{1,0:T(8,128)S(1)} %get-tuple-element.226, f32[16,27,128]{2,1,0:T(8,128)S(1)} %get-tuple-element.227, f32[16,128]{1,0:T(8,128)S(1)} %get-tuple-element.228, ...), kind=kLoop, calls=%fused_computation.16.clone.1 | loop fusion | flops 77854720 | bytes 917504 | tf_op jit(solution)/shard_map/while/body/eval_jaxpr/reduce_sum | solution.py:130
  408.6 12.3 %multiply_reduce_fusion.2 = f32[16,128]{1,0:T(8,128)S(1)} fusion(f32[16,27,128]{2,1,0:T(8,128)S(1)} %reshape.304, f32[16,27,128]{2,1,0:T(8,128)S(1)} %get-tuple-element.225, f32[16,128]{1,0:T(8,128)S(1)} %get-tuple-element.226, f32[16,27,128]{2,1,0:T(8,128)S(1)} %get-tuple-element.227, f32[16,128]{1,0:T(8,128)S(1)} %get-tuple-element.228, ...), kind=kLoop, calls=%fused_computation.16.clone.1 | loop fusion | flops 77854720 | bytes 917504 | tf_op jit(solution)/shard_map/while/body/eval_jaxpr/reduce_sum | solution.py:130
  426.9 12.3 %multiply_reduce_fusion.2 = f32[16,128]{1,0:T(8,128)S(1)} fusion(f32[16,27,128]{2,1,0:T(8,128)S(1)} %reshape.304, f32[16,27,128]{2,1,0:T(8,128)S(1)} %get-tuple-element.225, f32[16,128]{1,0:T(8,128)S(1)} %get-tuple-element.226, f32[16,27,128]{2,1,0:T(8,128)S(1)} %get-tuple-element.227, f32[16,128]{1,0:T(8,128)S(1)} %get-tuple-element.228, ...), kind=kLoop, calls=%fused_computation.16.clone.1 | loop fusion | flops 77854720 | bytes 917504 | tf_op jit(solution)/shard_map/while/body/eval_jaxpr/reduce_sum | solution.py:130
  445.2 12.3 %multiply_reduce_fusion.2 = f32[16,128]{1,0:T(8,128)S(1)} fusion(f32[16,27,128]{2,1,0:T(8,128)S(1)} %reshape.304, f32[16,27,128]{2,1,0:T(8,128)S(1)} %get-tuple-element.225, f32[16,128]{1,0:T(8,128)S(1)} %get-tuple-element.226, f32[16,27,128]{2,1,0:T(8,128)S(1)} %get-tuple-element.227, f32[16,128]{1,0:T(8,128)S(1)} %get-tuple-element.228, ...), kind=kLoop, calls=%fused_computation.16.clone.1 | loop fusion | flops 77854720 | bytes 917504 | tf_op jit(solution)/shard_map/while/body/eval_jaxpr/reduce_sum | solution.py:130
  463.7 7.9 collective-permute-start
  474.9 307.3 %while.20 = (s32[]{:T(128)}, f32[8,32,256]{2,1,0:T(8,128)S(1)}, s32[8,32,189]{2,1,0:T(8,128)S(1)}, s32[8,32,189]{2,1,0:T(8,128)}, bf16[2304,256]{1,0:T(8,128)(2,1)S(1)}, /*index=5*/bf16[16384,256]{1,0:T(8,128)(2,1)}, s32[]{:T(128)}) while((s32[]{:T(128)}, f32[8,32,256]{2,1,0:T(8,128)S(1)}, s32[8,32,189]{2,1,0:T(8,128)S(1)}, ...), condition=%wide.region_1.2_spmd, body=%wide.region_0.1_spmd.sunk | while | flops 467551968 | bytes 28340960 | solution.py:108
  475.8 24.9 %gather_fusion = bf16[6048,256]{1,0:T(8,128)(2,1)} fusion(bf16[2304,256]{1,0:T(8,128)(2,1)S(1)} %get-tuple-element.249, s32[6144]{0:T(1024)S(1)} %pad_clamp_fusion.6), kind=kCustom, calls=%fused_computation.clone.1 | custom fusion | bytes 6217344 | tf_op jit(solution)/shard_map/while/body/eval_jaxpr/gather | solution.py:97
  500.8 4.5 reshape.298
  508.4 4.9 fusion.38
  514.3 24.9 %gather_fusion = bf16[6048,256]{1,0:T(8,128)(2,1)} fusion(bf16[2304,256]{1,0:T(8,128)(2,1)S(1)} %get-tuple-element.249, s32[6144]{0:T(1024)S(1)} %pad_clamp_fusion.6), kind=kCustom, calls=%fused_computation.clone.1 | custom fusion | bytes 6217344 | tf_op jit(solution)/shard_map/while/body/eval_jaxpr/gather | solution.py:97
  539.2 4.5 reshape.298
  546.8 4.9 fusion.38
  552.7 24.9 %gather_fusion = bf16[6048,256]{1,0:T(8,128)(2,1)} fusion(bf16[2304,256]{1,0:T(8,128)(2,1)S(1)} %get-tuple-element.249, s32[6144]{0:T(1024)S(1)} %pad_clamp_fusion.6), kind=kCustom, calls=%fused_computation.clone.1 | custom fusion | bytes 6217344 | tf_op jit(solution)/shard_map/while/body/eval_jaxpr/gather | solution.py:97
  577.6 4.5 reshape.298
  585.2 4.9 fusion.38
  591.1 24.9 %gather_fusion = bf16[6048,256]{1,0:T(8,128)(2,1)} fusion(bf16[2304,256]{1,0:T(8,128)(2,1)S(1)} %get-tuple-element.249, s32[6144]{0:T(1024)S(1)} %pad_clamp_fusion.6), kind=kCustom, calls=%fused_computation.clone.1 | custom fusion | bytes 6217344 | tf_op jit(solution)/shard_map/while/body/eval_jaxpr/gather | solution.py:97
  616.0 4.5 reshape.298
  623.6 4.9 fusion.38
  629.5 24.9 %gather_fusion = bf16[6048,256]{1,0:T(8,128)(2,1)} fusion(bf16[2304,256]{1,0:T(8,128)(2,1)S(1)} %get-tuple-element.249, s32[6144]{0:T(1024)S(1)} %pad_clamp_fusion.6), kind=kCustom, calls=%fused_computation.clone.1 | custom fusion | bytes 6217344 | tf_op jit(solution)/shard_map/while/body/eval_jaxpr/gather | solution.py:97
  654.5 4.5 reshape.298
  662.1 4.9 fusion.38
  667.9 24.9 %gather_fusion = bf16[6048,256]{1,0:T(8,128)(2,1)} fusion(bf16[2304,256]{1,0:T(8,128)(2,1)S(1)} %get-tuple-element.249, s32[6144]{0:T(1024)S(1)} %pad_clamp_fusion.6), kind=kCustom, calls=%fused_computation.clone.1 | custom fusion | bytes 6217344 | tf_op jit(solution)/shard_map/while/body/eval_jaxpr/gather | solution.py:97
  692.9 4.5 reshape.298
  700.5 4.9 fusion.38
  706.3 24.9 %gather_fusion = bf16[6048,256]{1,0:T(8,128)(2,1)} fusion(bf16[2304,256]{1,0:T(8,128)(2,1)S(1)} %get-tuple-element.249, s32[6144]{0:T(1024)S(1)} %pad_clamp_fusion.6), kind=kCustom, calls=%fused_computation.clone.1 | custom fusion | bytes 6217344 | tf_op jit(solution)/shard_map/while/body/eval_jaxpr/gather | solution.py:97
  731.3 4.5 reshape.298
  738.9 4.9 fusion.38
  744.8 24.9 %gather_fusion = bf16[6048,256]{1,0:T(8,128)(2,1)} fusion(bf16[2304,256]{1,0:T(8,128)(2,1)S(1)} %get-tuple-element.249, s32[6144]{0:T(1024)S(1)} %pad_clamp_fusion.6), kind=kCustom, calls=%fused_computation.clone.1 | custom fusion | bytes 6217344 | tf_op jit(solution)/shard_map/while/body/eval_jaxpr/gather | solution.py:97
  777.3 4.9 fusion.38
  (306 shorter events, 162.0 us)
Async XLA Ops:
  7.2 1.2 copy-start
  7.2 4.4 copy-start.3
  7.2 16.5 %copy-start.6 = (s32[128,16]{0,1:T(8,128)S(1)}, s32[128,16]{0,1:T(8,128)}, u32[]{:S(2)}) copy-start(s32[128,16]{0,1:T(8,128)} %param.24) | copy-start | bytes 24580
  7.2 16.7 %copy-start.2 = (f32[256,3,128]{2,0,1:T(8,128)S(1)}, f32[256,3,128]{2,0,1:T(8,128)}, u32[]{:S(2)}) copy-start(f32[256,3,128]{2,0,1:T(8,128)} %param.18) | copy-start | bytes 1179652
  7.2 148.3 %all-reduce.2.cloned.1.call-start = ((), (), s32[]{:S(2)}) async-start(), calls=%async_computation.3 | async-start | bytes 131072 | tf_op jit(solution)/shard_map/psum | solution.py:74
  13.3 20.6 %all-to-all-start.2 = ((f32[128,4,128]{2,1,0:T(4,128)}), f32[128,4,128]{2,1,0:T(4,128)S(1)}, u32[]{:S(2)}, u32[]{:S(2)}) async-start(f32[128,4,128]{2,1,0:T(4,128)} %bitcast.25), calls=%async_computation.2 | async-start | bytes 524288 | tf_op jit(solution)/shard_map/all_to_all | solution.py:61
  23.9 3.3 copy-start.7
  26.2 19.3 %copy-start.1 = (bf16[256,256]{1,0:T(8,128)(2,1)S(1)}, bf16[256,256]{1,0:T(8,128)(2,1)}, u32[]{:S(2)}) copy-start(bf16[256,256]{1,0:T(8,128)(2,1)} %param.17) | copy-start | bytes 393220
  33.8 122.7 %all-to-all-start.1 = ((f32[128,4,3,128]{3,1,2,0:T(4,128)}), f32[128,4,3,128]{3,1,2,0:T(4,128)S(1)}, u32[]{:S(2)}, u32[]{:S(2)}) async-start(f32[128,4,3,128]{3,1,2,0:T(4,128)} %copy.116), calls=%async_computation.1 | async-start | bytes 1572864 | tf_op jit(solution)/shard_map/all_to_all | solution.py:60
  45.6 9.0 %copy-start.4 = (s32[256,27]{0,1:T(8,128)S(1)}, s32[256,27]{0,1:T(8,128)}, u32[]{:S(2)}) copy-start(s32[256,27]{0,1:T(8,128)} %param.28) | copy-start | bytes 82948
  45.6 109.9 %copy-start.5 = (f32[64,64]{1,0:T(8,128)S(1)}, f32[64,64]{1,0:T(8,128)}, u32[]{:S(2)}) copy-start(f32[64,64]{1,0:T(8,128)} %param.23) | copy-start | bytes 49156
  156.6 317.0 %all-to-all-start = ((bf16[128,16,256]{2,1,0:T(8,128)(2,1)}), bf16[128,16,256]{2,1,0:T(8,128)(2,1)}, u32[]{:S(2)}, u32[]{:S(2)}) async-start(bf16[128,16,256]{2,1,0:T(8,128)(2,1)} %bitcast.15), calls=%async_computation | async-start | bytes 2097152 | tf_op jit(solution)/shard_map/all_to_all | solution.py:58
  458.1 16.8 %copy-start.8 = (f32[8,32,256]{2,1,0:T(8,128)S(1)}, f32[8,32,256]{2,1,0:T(8,128)}, u32[]{:S(2)}) copy-start(f32[8,32,256]{2,1,0:T(8,128)} %custom-call.14) | copy-start | bytes 786436
  460.9 10.9 %collective-permute-start.1 = (f32[8,5,128]{2,1,0:T(8,128)S(1)}, f32[8,5,128]{2,1,0:T(8,128)S(1)}, u32[]{:S(2)}, u32[]{:S(2)}) collective-permute-start(f32[8,5,128]{2,1,0:T(8,128)S(1)} %broadcast_select_fusion), channel_id=1, source_target_pairs={{0,1},{1,2},{2,3},{3,4},{4,5},{5,6},{6,7},{7,8},{8,9},{9,10},{10,1... | collective-permute-start | bytes 61448 | tf_op jit(solution)/shard_map/ppermute | solution.py:18
  463.7 9.3 %collective-permute-start = (f32[8,5,128]{2,1,0:T(8,128)S(1)}, f32[8,5,128]{2,1,0:T(8,128)S(1)}, u32[]{:S(2)}, u32[]{:S(2)}) collective-permute-start(f32[8,5,128]{2,1,0:T(8,128)S(1)} %slice_select_fusion), channel_id=1, source_target_pairs={{1,0},{2,1},{3,2},{4,3},{5,4},{6,5},{7,6},{8,7},{9,8},{10,9},{11,1... | collective-permute-start | bytes 61448 | tf_op jit(solution)/shard_map/ppermute | solution.py:18
Sparse Core Ops, SparseCore 0:
  12.8 142.6 all-reduce.1
where the time goes:
time: 795 us; the launch traced here: 792 us
  local copies, waits for them, and re-layouts  349 us (44%)
  other arithmetic  222 us (28%)
  waiting for transfers between devices  107 us (13%)
  matrix products  65.1 us (8%)
  starting transfers between devices  32.4 us (4%)
  between operations  14.3 us (2%)
    gather x16, local copies, waits for them, and re-layouts, translate_block(): picked = source_table[source_ids]  236 us
    reduce_sum x16, other arithmetic, one_block(): return jnp.sum(kernel * picked_charge[:, :, None, :], axis=(1, 3))  197 us
    psum x1, waiting for transfers between devices, per_device(): top_sums = lax.psum(partial_value, ('leaf', 'sub'))  100 us
    gather x16, local copies, waits for them, and re-layouts, one_block(): picked_pos = pos_table[near_list]  44.3 us
    dot_general x8, matrix products, translate_block(): jnp.dot(grouped.reshape(source_ids.shape[0], -1), ops_flat, preferred_ele...  39.6 us
    dot_general x8, matrix products, translate_block(): jnp.einsum('cjk,cjf->ckf', one_hot, picked, preferred_element_type=jnp.fl...  19.6 us
    gather x32, local copies, waits for them, and re-layouts, one_block(): picked_charge = charge_table[near_list]  18.8 us
  transfers between devices with their start and end apart: 6, of which 3 were waited for; matrix products, arithmetic and copies ran while one was open for 41% of the time, Pallas kernels for 0%

commit v1 on v0

v1 whole, which is shorter than its diff:
```python
import functools

import jax
import jax.numpy as jnp
from jax import lax
from jax.experimental import pallas as pl
from jax.experimental.pallas import tpu as pltpu
from jax.sharding import PartitionSpec as P

F32 = jnp.float32
BF16 = jnp.bfloat16
MCAP = 8
SOFTENING = 0.01
AXES = ("leaf", "sub")
LANES = 128
FEAT = 32
UNROLL = 8
KSTEP = 8


def shifted(x, axis, by):
    devices = lax.axis_size(axis)
    pairs = [(i, i + by) for i in range(devices) if 0 <= i + by < devices]
    return lax.ppermute(x, axis, pairs)


def pieces(x, count):
    out = []
    for _ in range(count):
        head = x.astype(BF16).astype(F32)
        out.append(head)
        x = x - head
    return out


def main_kernel(
    src_ref,
    near_ref,
    op_ref,
    own_ref,
    got_ref,
    ownp_ref,
    gotp_ref,
    far_ref,
    tr_hbm,
    local_ref,
    pot_ref,
    tab,
    charge,
    target,
    source,
    group_lo,
    group_hi,
    tr_ref,
    tr_sem,
    *picked,
    list_width,
    op_count,
    pitch,
):
    cells = own_ref.shape[0]
    near_count = near_ref.shape[1]
    list_pad = op_ref.shape[1]
    tr_copy = pltpu.make_async_copy(tr_hbm, tr_ref, tr_sem)
    tr_copy.start()
    for buf in picked:
        buf[...] = jnp.zeros_like(buf)

    def spread(ref, base):
        def step(i, carry):
            rows = ref[pl.ds(pl.multiple_of(i * 16, 16), 16), :].astype(F32)
            at = base + i * 32
            tab[pl.ds(at, 16, stride=2), :] = rows[:, :LANES]
            tab[pl.ds(at + 1, 16, stride=2), :] = rows[:, LANES:]
            return carry

        lax.fori_loop(0, ref.shape[0] // 16, step, 0)

    spread(own_ref, 0)
    spread(got_ref, 2 * cells)

    group_lo[...] = jnp.zeros_like(group_lo)
    group_hi[...] = jnp.zeros_like(group_hi)

    def features(ref, first, stage, is_target):
        def step(i, carry):
            at = pl.multiple_of(i * 8, 8)
            axes = [pieces(ref[a, pl.ds(at, 8), :] - 0.5, 2) for a in range(3)]
            norm = jnp.zeros((8, LANES), F32)
            for high, low in axes:
                norm = norm + (high + low) * (high + low)
            one = jnp.ones((8, LANES), F32)
            highs = [a[0] for a in axes]
            lows = [a[1] for a in axes]
            if is_target:
                twice = [-2.0 * h for h in highs], [-2.0 * v for v in lows]
                rows = twice[0] * 2 + twice[1] * 2 + pieces(norm, 3) + [one] * 3
            else:
                rows = (highs + lows) * 2 + [one] * 3 + pieces(norm + SOFTENING, 3)
                charge[pl.ds(first + at, 8), :] = ref[3, pl.ds(at, 8), :]
            for k, row in enumerate(rows):
                stage[pl.ds(at * FEAT + k, 8, stride=FEAT), :] = row
            return carry

        lax.fori_loop(0, ref.shape[1] // 8, step, 0)

    def packed(stage, out, first, count):
        def step(i, carry):
            out[first + i] = stage[pl.ds(pl.multiple_of(i * FEAT, FEAT), FEAT), :].astype(BF16)
            return carry

        lax.fori_loop(0, count, step, 0)

    features(ownp_ref, 0, group_lo, True)
    packed(group_lo, target, 0, cells)
    features(ownp_ref, 0, group_hi, False)
    packed(group_hi, source, 0, cells)
    features(gotp_ref, cells, group_lo, False)
    packed(group_lo, source, cells, gotp_ref.shape[1])

    op_ids = lax.broadcasted_iota(jnp.int32, (op_count, list_pad), 0)

    def group(cell, buf):
        low = buf[pl.ds(0, list_pad, stride=2), :].astype(BF16)
        high = buf[pl.ds(1, list_pad, stride=2), :].astype(BF16)
        hot = jnp.where(op_ids == op_ref[pl.ds(cell, 1), :], 1.0, 0.0).astype(BF16)
        out = jnp.dot(hot, jnp.concatenate([low, high], 1), preferred_element_type=F32)
        group_lo[pl.ds(cell, op_count, stride=pitch), :] = out[:, :LANES]
        group_hi[pl.ds(cell, op_count, stride=pitch), :] = out[:, LANES:]

    def reduced(total, cell):
        pot_ref[pl.ds(cell, 1), :] = jnp.sum(total.T, axis=0, keepdims=True)

    per_pair = -(-list_width // ((near_count + 1) // 2))

    def leaves(c, carry):
        pending = None
        for u in range(UNROLL):
            cell = c * UNROLL + u
            x = target[cell]
            total = jnp.zeros((LANES, LANES), F32)
            taken = 0
            for p in range(0, near_count, 2):
                for j in range(taken, min(taken + per_pair, list_width)):
                    row = pl.multiple_of(src_ref[cell, j], 2)
                    picked[u][2 * j : 2 * j + 2, :] = tab[pl.ds(row, 2), :]
                taken += per_pair
                ids = [near_ref[cell, n] for n in range(p, min(p + 2, near_count))]
                y = [source[i] for i in ids]
                y = jnp.concatenate(y, axis=1) if len(y) > 1 else y[0]
                dist = lax.dot_general(
                    x, y, (((0,), (0,)), ((), ())), preferred_element_type=F32
                )
                for t, i in enumerate(ids):
                    part = lax.rsqrt(dist[:, t * LANES : (t + 1) * LANES])
                    total = total + part * charge[pl.ds(i, 1), :]
                if p == 4:
                    group(jnp.maximum(cell - 1, 0), picked[(u - 1) % UNROLL])
                if p == 8 and pending is not None:
                    reduced(*pending)
            pending = (total, cell)
        reduced(*pending)
        return carry

    lax.fori_loop(0, cells // UNROLL, leaves, 0)
    group(cells - 1, picked[UNROLL - 1])

    tr_copy.wait()
    far = jnp.concatenate([far_ref[...]] * (cells // 8), 0)
    local_ref[...] = far
    width = 2 * LANES

    def translate(k, carry):
        parts = []
        for kk in range(KSTEP):
            at = pl.ds(pl.multiple_of((k * KSTEP + kk) * pitch, 8), cells)
            parts += [group_lo[at, :].astype(BF16), group_hi[at, :].astype(BF16)]
        ops = tr_ref[pl.ds(k * KSTEP, KSTEP)].reshape(KSTEP * width, width)
        local_ref[...] += jnp.dot(
            jnp.concatenate(parts, 1), ops, preferred_element_type=F32
        )
        return carry

    lax.fori_loop(0, op_count // KSTEP, translate, 0)


def main_call(src, near, ops, own, got, own_p, got_p, far, translate_ops):
    cells = own.shape[0]
    list_width = src.shape[1]
    list_pad = ops.shape[1]
    op_count = translate_ops.shape[0]
    tables = cells + got_p.shape[1]
    pitch = cells + 8
    smem = pl.BlockSpec(memory_space=pltpu.SMEM)
    vmem = pl.BlockSpec(memory_space=pltpu.VMEM)
    return pl.pallas_call(
        functools.partial(
            main_kernel, list_width=list_width, op_count=op_count, pitch=pitch
        ),
        out_shape=(
            jax.ShapeDtypeStruct((cells, 2 * LANES), F32),
            jax.ShapeDtypeStruct((cells, LANES), F32),
        ),
        in_specs=[smem, smem] + [vmem] * 6 + [pl.BlockSpec(memory_space=pl.ANY)],
        out_specs=(vmem, vmem),
        scratch_shapes=[
            pltpu.VMEM((2 * (cells + got.shape[0]), LANES), F32),
            pltpu.VMEM((tables, LANES), F32),
            pltpu.VMEM((cells, FEAT, LANES), BF16),
            pltpu.VMEM((tables, FEAT, LANES), BF16),
            pltpu.VMEM((op_count * pitch, LANES), F32),
            pltpu.VMEM((op_count * pitch, LANES), F32),
            pltpu.VMEM(translate_ops.shape, BF16),
            pltpu.SemaphoreType.DMA,
        ]
        + [pltpu.VMEM((2 * list_pad, LANES), F32)] * UNROLL,
        compiler_params=pltpu.CompilerParams(vmem_limit_bytes=60 * 1024 * 1024),
    )(src, near, ops, own, got, own_p, got_p, far, translate_ops)


def per_device(
    multipole,
    positions,
    charges,
    translate_ops,
    upward_ops,
    downward_ops,
    top_weight,
    send_cells,
    send_leaves,
    list_source,
    list_operator,
    near_leaves,
    move_counts,
):
    highest = lax.Precision.HIGHEST
    cells, width = multipole.shape
    leaf_size = positions.shape[2]
    ranks = lax.axis_size(AXES)
    rank = lax.axis_index(AXES)
    tops = top_weight.shape[0]

    octants = jnp.sum(multipole.astype(F32).reshape(cells // 8, 8, width), axis=0)
    share = jnp.dot(
        octants.reshape(1, 8 * width),
        upward_ops.astype(F32).reshape(8 * width, width),
        precision=highest,
        preferred_element_type=F32,
    )

    body = jnp.concatenate([positions, charges[:, None, :]], 1)
    sent = body[send_leaves].reshape(ranks, -1, leaf_size)
    share_rows = jnp.broadcast_to(share.reshape(1, 2, leaf_size), (ranks, 2, leaf_size))
    sent = jnp.concatenate([sent, share_rows], 1)
    got = lax.all_to_all(sent, AXES, split_axis=0, concat_axis=0, tiled=True)

    pick = (send_cells.reshape(-1, 1) == jnp.arange(cells, dtype=jnp.int32)[None, :])
    out_cells = jnp.dot(pick.astype(BF16), multipole, preferred_element_type=F32)
    out_cells = out_cells.astype(BF16).reshape(ranks, -1, width)
    got_cells = lax.all_to_all(out_cells, AXES, split_axis=0, concat_axis=0, tiled=True)

    shares = got[:, -2:, :].reshape(tops, ranks // tops, width)
    top_sums = jnp.sum(shares, axis=1)
    top = rank * tops // ranks
    weight = lax.dynamic_slice_in_dim(top_weight, top, 1, 0)
    coarse = jnp.dot(weight, top_sums, precision=highest, preferred_element_type=F32)
    coarse = jnp.broadcast_to(coarse.astype(BF16)[None], (8, 1, width))
    far = lax.dot_general(
        coarse, downward_ops, (((2,), (1,)), ((0,), (0,))), preferred_element_type=F32
    ).reshape(8, width)

    own_p = jnp.transpose(body, (1, 0, 2))
    got_p = got[:, :-2, :].reshape(-1, 4, leaf_size)
    got_p = jnp.transpose(got_p, (1, 0, 2))
    list_pad = -(-list_operator.shape[1] // 64) * 64
    ops = jnp.pad(
        list_operator,
        ((0, 0), (0, list_pad - list_operator.shape[1])),
        constant_values=translate_ops.shape[0],
    )
    local_exp, potential = main_call(
        list_source * 2,
        near_leaves,
        ops,
        multipole,
        got_cells.reshape(-1, width),
        own_p,
        got_p,
        far,
        translate_ops,
    )

    def payload(a, b):
        return jnp.concatenate([body[a:b], potential[a:b, None, :]], 1)

    slot = jnp.arange(MCAP, dtype=jnp.int32)
    lower = jnp.where((slot < move_counts[0, 0])[:, None, None], payload(0, MCAP), 0.0)
    upper = payload(cells - MCAP, cells)[::-1]
    upper = jnp.where((slot < move_counts[0, 1])[:, None, None], upper, 0.0)
    from_upper = shifted(lower, AXES, -1)
    from_lower = shifted(upper, AXES, 1)
    arrivals = jnp.concatenate([from_upper, from_lower], 0)
    return (local_exp, potential, arrivals)


def solution(mesh):
    rows = P(AXES, None)
    blocks = P(AXES, None, None)
    placed = (rows, blocks, rows) + (P(),) * 4 + (rows,) * 6
    return jax.shard_map(
        per_device,
        mesh=mesh,
        in_specs=placed,
        out_specs=(rows, rows, blocks),
        check_vma=False,
    )
```

time: 795 us -> 222 us (0.28)
  local copies, waits for them, and re-layouts: 349 us -> 8.86 us
  other arithmetic: 222 us -> 6.3 us
  Pallas kernels: 0 us -> 141 us
  waiting for transfers between devices: 107 us -> 33.1 us
  matrix products: 65.1 us -> 4.34 us
  between operations: 14.3 us -> 0.92 us
    gather x69 -> x1, local copies, waits for them, and re-layouts: 313 us -> 2.07 us  [per_device(): sent = body[send_leaves].reshape(ranks, -1, leaf_size)]
    reduce_sum x16 -> x2, other arithmetic: 197 us -> 0.19 us  [the longest x1 0.16 us: per_device(): top_sums = jnp.sum(shares, axis=1)]
    pallas_call x0 -> x1, Pallas kernels: none -> 141 us  [main_call(): pl.pallas_call(functools.partial(main_kernel, list_width=list_width, op_c...]
    psum x1 -> x0, waiting for transfers between devices: 100 us -> none  [per_device(): top_sums = lax.psum(partial_value, ('leaf', 'sub'))]
    dot_general x21 -> x4, matrix products: 65.1 us -> 4.34 us  [the longest x1 1.74 us: per_device(): jnp.dot(octants.reshape(1, 8 * width), upward_ops.astype(F32).reshape(8 *...]
    all_to_all x3 -> x2, waiting for transfers between devices: 6 us -> 31.7 us  [the longest x1 18.8 us: per_device(): got = lax.all_to_all(sent, AXES, split_axis=0, concat_axis=0, tiled=True)]
    select_n x30 -> x3, other arithmetic: 19.5 us -> 0.15 us  [the longest x1 0.08 us: per_device(): upper = jnp.where((slot < move_counts[0, 1])[:, None, None], upper, 0.0)]
    dynamic_update_slice x16 -> x0, local copies, waits for them, and re-layouts: 9.69 us -> none  [per_device(): lax.map(one_block, (positions.reshape(-1, block_size, 3, leaf_size), near...]
  transfers between devices with their start and end apart: 6 -> 4, of which waited for: 3 -> 3; matrix products, arithmetic and copies ran while one was open for 41% -> 5% of each run, Pallas kernels for 0% -> 0%
where the time goes in v1:
time: 222 us; the launch traced here: 221 us
  Pallas kernels  141 us (64%)
  waiting for transfers between devices  33.1 us (15%)
  starting transfers between devices  26.6 us (12%)
  local copies, waits for them, and re-layouts  8.86 us (4%)
  other arithmetic  6.3 us (3%)
  matrix products  4.34 us (2%)
    pallas_call x1, Pallas kernels, main_call(): pl.pallas_call(functools.partial(main_kernel, list_width=list_width, op_c...  141 us
    all_to_all x1, waiting for transfers between devices, per_device(): got = lax.all_to_all(sent, AXES, split_axis=0, concat_axis=0, tiled=True)  18.8 us
    all_to_all x1, waiting for transfers between devices, per_device(): lax.all_to_all(out_cells, AXES, split_axis=0, concat_axis=0, tiled=True)  12.8 us
    all_to_all x1, starting transfers between devices, per_device(): got = lax.all_to_all(sent, AXES, split_axis=0, concat_axis=0, tiled=True)  10.4 us
    ppermute x2, starting transfers between devices, shifted(): return lax.ppermute(x, axis, pairs)  9.76 us
    all_to_all x1, starting transfers between devices, per_device(): lax.all_to_all(out_cells, AXES, split_axis=0, concat_axis=0, tiled=True)  6.45 us
  transfers between devices with their start and end apart: 4, of which 3 were waited for; matrix products, arithmetic and copies ran while one was open for 5% of the time, Pallas kernels for 0%

profile of v1, /device:TPU:8, one launch (start us, length us, event | category | flops | bytes accessed | tf_op | source)
XLA Modules:
  0.0 221.2 jit_solution(9296000143157383352)
XLA Ops:
  0.6 0.0 copy-start
  0.6 0.0 copy-start.7
  0.7 0.0 copy-start.2
  0.7 2.0 pad_maximum_fusion.1
  2.7 0.3 copy.31
  3.0 0.0 copy-done.7
  3.1 0.1 copy.30
  3.2 0.1 reshape.83
  3.3 0.0 copy-done.2
  3.4 2.1 gather_fusion
  5.4 1.7 fusion
  7.2 1.3 pad_maximum_fusion
  8.5 10.4 %all-to-all-start.1 = ((f32[128,18,128]{2,1,0:T(8,128)}), f32[128,18,128]{2,1,0:T(8,128)S(1)}, u32[]{:S(2)}, u32[]{:S(2)}) async-start(f32[128,18,128]{2,1,0:T(8,128)} %pad_maximum_fusion), calls=%async_computation.1 | async-start | bytes 3145728 | tf_op jit(solution)/shard_map/all_to_all | solution.py:255
  19.0 0.0 copy-start.5
  19.0 0.0 copy-start.8
  19.0 0.0 copy-done.6
  19.0 0.1 copy.29
  19.1 0.1 eq.15
  19.2 0.0 copy-done.4
  19.2 0.1 copy.26
  19.4 1.1 copy.28
  20.4 0.8 pad.4.op_ref
  21.2 0.8 copy.33.near_ref
  21.9 0.6 fusion.13
  22.5 1.5 convolution_convert_fusion
  24.1 18.8 %all-to-all-done.1 = f32[128,18,128]{2,1,0:T(8,128)S(1)} async-done(((f32[128,18,128]{2,1,0:T(8,128)}), f32[128,18,128]{2,1,0:T(8,128)S(1)}, u32[]{:S(2)}, u32[]{:S(2)}) %all-to-all-start.1) | async-done | bytes 1179680 | tf_op jit(solution)/shard_map/all_to_all | solution.py:255
  42.9 6.4 %all-to-all-start = ((bf16[128,16,256]{2,1,0:T(8,128)(2,1)}), bf16[128,16,256]{2,1,0:T(8,128)(2,1)}, u32[]{:S(2)}, u32[]{:S(2)}) async-start(bf16[128,16,256]{2,1,0:T(8,128)(2,1)} %bitcast.44), calls=%async_computation | async-start | bytes 2097152 | tf_op jit(solution)/shard_map/all_to_all | solution.py:260
  49.3 0.7 iota_compare_fusion.2
  50.0 0.7 iota_compare_fusion.3
  50.7 0.7 broadcast_multiply_fusion.src_ref
  51.4 0.2 reshape.78
  51.6 0.2 reduce_sum.19
  51.8 0.8 fusion.8
  52.6 0.0 copy-done
  52.6 0.2 fusion.6
  52.9 0.6 copy.47
  53.5 0.1 slice.34
  53.6 1.1 copy.46
  54.6 12.8 %all-to-all-done = bf16[128,16,256]{2,1,0:T(8,128)(2,1)} async-done(((bf16[128,16,256]{2,1,0:T(8,128)(2,1)}), bf16[128,16,256]{2,1,0:T(8,128)(2,1)}, u32[]{:S(2)}, u32[]{:S(2)}) %all-to-all-start) | async-done | bytes 1048608 | tf_op jit(solution)/shard_map/all_to_all | solution.py:260
  67.5 141.0 %shard_map.148 = (f32[256,256]{1,0:T(8,128)}, f32[256,128]{1,0:T(8,128)}) custom-call(s32[256,189]{1,0:T(8,128)} %broadcast_multiply_fusion.src_ref, s32[256,27]{1,0:T(8,128)} %copy.33.near_ref, s32[256,192]{1,0:T(8,128)} %pad.4.op_ref, bf16[256,256]{1,0:T(8,128)(2,1)} %own_ref.1, bf16[2048,256]{1,0:T(8,128)(2,1)} %bitcast.1.got_ref, ...), custom_call_target="tpu_custom_call" | custom-call | tf_op jit(solution)/shard_map/pallas_call | solution.py:196
  208.4 0.7 slice_bitcast_fusion.1
  209.2 0.1 broadcast_select_fusion
  209.2 1.9 collective-permute-start.1
  211.2 0.1 maximum_select_fusion
  211.2 7.8 %collective-permute-start = (f32[8,5,128]{2,0,1:T(8,128)S(1)}, f32[8,5,128]{2,0,1:T(8,128)S(1)}, u32[]{:S(2)}, u32[]{:S(2)}) collective-permute-start(f32[8,5,128]{2,0,1:T(8,128)S(1)} %maximum_select_fusion), channel_id=1, source_target_pairs={{1,0},{2,1},{3,2},{4,3},{5,4},{6,5},{7,6},{8,7},{9,8},{10,9},{11,1... | collective-permute-start | bytes 61448 | tf_op jit(solution)/shard_map/ppermute | solution.py:24
  219.1 0.0 collective-permute-done.1
  219.1 1.4 collective-permute-done
  220.6 0.6 pad_maximum_fusion.2
  (18 shorter events, 0.2 us)
Async XLA Ops:
  0.6 52.0 %copy-start = (bf16[8,256,256]{2,1,0:T(8,128)(2,1)S(1)}, bf16[8,256,256]{2,1,0:T(8,128)(2,1)}, u32[]{:S(2)}) copy-start(bf16[8,256,256]{2,1,0:T(8,128)(2,1)} %param.18) | copy-start | bytes 3145732
  0.6 2.4 %copy-start.7 = (s32[128,4]{0,1:T(4,128)S(1)}, s32[128,4]{0,1:T(4,128)}, u32[]{:S(2)}) copy-start(s32[128,4]{0,1:T(4,128)} %param.21) | copy-start | bytes 6148
  0.7 2.6 %copy-start.2 = (bf16[256,256]{1,0:T(8,128)(2,1)S(1)}, bf16[256,256]{1,0:T(8,128)(2,1)}, u32[]{:S(2)}) copy-start(bf16[256,256]{1,0:T(8,128)(2,1)} %own_ref.1) | copy-start | bytes 393220
  8.5 10.5 %copy-start.6 = (s32[128,16]{0,1:T(8,128)S(1)}, s32[128,16]{0,1:T(8,128)}, u32[]{:S(2)}) copy-start(s32[128,16]{0,1:T(8,128)} %param.20) | copy-start | bytes 24580
  8.5 10.7 %copy-start.4 = (s32[256,189]{0,1:T(8,128)S(1)}, s32[256,189]{0,1:T(8,128)}, u32[]{:S(2)}) copy-start(s32[256,189]{0,1:T(8,128)} %param.22) | copy-start | bytes 580612
  8.5 34.4 %all-to-all-start.1 = ((f32[128,18,128]{2,1,0:T(8,128)}), f32[128,18,128]{2,1,0:T(8,128)S(1)}, u32[]{:S(2)}, u32[]{:S(2)}) async-start(f32[128,18,128]{2,1,0:T(8,128)} %pad_maximum_fusion), calls=%async_computation.1 | async-start | bytes 3145728 | tf_op jit(solution)/shard_map/all_to_all | solution.py:255
  19.0 2.2 copy-start.5
  19.0 3.0 %copy-start.8 = (s32[1,2]{1,0:T(1,128)S(1)}, s32[1,2]{1,0:T(1,128)}, u32[]{:S(2)}) copy-start(s32[1,2]{1,0:T(1,128)} %param.25) | copy-start | bytes 28
  22.5 28.1 %copy-start.1 = (f32[256,3,128]{2,0,1:T(8,128)S(1)}, f32[256,3,128]{2,0,1:T(8,128)}, u32[]{:S(2)}) copy-start(f32[256,3,128]{2,0,1:T(8,128)} %param.14) | copy-start | bytes 1179652
  22.5 28.1 %copy-start.3 = (f32[256,128]{1,0:T(8,128)S(1)}, f32[256,128]{1,0:T(8,128)}, u32[]{:S(2)}) copy-start(f32[256,128]{1,0:T(8,128)} %param.15) | copy-start | bytes 393220
  42.9 24.6 %all-to-all-start = ((bf16[128,16,256]{2,1,0:T(8,128)(2,1)}), bf16[128,16,256]{2,1,0:T(8,128)(2,1)}, u32[]{:S(2)}, u32[]{:S(2)}) async-start(bf16[128,16,256]{2,1,0:T(8,128)(2,1)} %bitcast.44), calls=%async_computation | async-start | bytes 2097152 | tf_op jit(solution)/shard_map/all_to_all | solution.py:260
  209.2 9.9 %collective-permute-start.1 = (f32[8,5,128]{2,0,1:T(8,128)S(1)}, f32[8,5,128]{2,0,1:T(8,128)S(1)}, u32[]{:S(2)}, u32[]{:S(2)}) collective-permute-start(f32[8,5,128]{2,0,1:T(8,128)S(1)} %broadcast_select_fusion), channel_id=1, source_target_pairs={{0,1},{1,2},{2,3},{3,4},{4,5},{5,6},{6,7},{7,8},{8,9},{9,10},{10,1... | collective-permute-start | bytes 61448 | tf_op jit(solution)/shard_map/ppermute | solution.py:24
  211.2 9.3 %collective-permute-start = (f32[8,5,128]{2,0,1:T(8,128)S(1)}, f32[8,5,128]{2,0,1:T(8,128)S(1)}, u32[]{:S(2)}, u32[]{:S(2)}) collective-permute-start(f32[8,5,128]{2,0,1:T(8,128)S(1)} %maximum_select_fusion), channel_id=1, source_target_pairs={{1,0},{2,1},{3,2},{4,3},{5,4},{6,5},{7,6},{8,7},{9,8},{10,9},{11,1... | collective-permute-start | bytes 61448 | tf_op jit(solution)/shard_map/ppermute | solution.py:24

commit v2 on v1

--- a/solution.py
+++ b/solution.py
@@ -33,9 +33,200 @@
     return out
 
 
+def partner(rank):
+    subs = lax.axis_size("sub")
+    return (rank // subs, lax.rem(rank, subs))
+
+
+def halves_in_rows(ref, out, base):
+    def step(i, carry):
+        rows = ref[pl.ds(pl.multiple_of(i * 16, 16), 16), :].astype(F32)
+        at = base + i * 32
+        out[pl.ds(at, 16, stride=2), :] = rows[:, :LANES]
+        out[pl.ds(at + 1, 16, stride=2), :] = rows[:, LANES:]
+        return carry
+
+    lax.fori_loop(0, ref.shape[0] // 16, step, 0, unroll=4)
+
+
+def pack_kernel(
+    cell_ids, leaf_ids, own_ref, body_ref, up_ref, out_cells, out_body, share, tab, stage
+):
+    ranks, cap, width = out_cells.shape
+    blocks = out_body.shape[1] // 4
+    halves_in_rows(own_ref, tab, 0)
+
+    def pick(r, carry):
+        for s in range(cap):
+            row = pl.multiple_of(cell_ids[r * cap + s], 2)
+            stage[pl.ds(r * 2 * cap + 2 * s, 2), :] = tab[pl.ds(row, 2), :]
+        for s in range(blocks):
+            row = pl.multiple_of(leaf_ids[r * blocks + s], 4)
+            out_body[r, 4 * s : 4 * s + 4, :] = body_ref[pl.ds(row, 4), :]
+        return carry
+
+    lax.fori_loop(0, ranks, pick, 0, unroll=2)
+
+    def pack(r, carry):
+        low = stage[pl.ds(r * 2 * cap, cap, stride=2), :]
+        high = stage[pl.ds(r * 2 * cap + 1, cap, stride=2), :]
+        out_cells[r] = jnp.concatenate([low, high], 1).astype(BF16)
+        return carry
+
+    lax.fori_loop(0, ranks, pack, 0, unroll=4)
+
+    rows = own_ref.shape[0]
+    octants = jnp.sum(own_ref[...].astype(F32).reshape(rows // 8, 8, width), axis=0)
+    lhs = jnp.concatenate(pieces(octants, 3) + [jnp.zeros((8, width), F32)], 0)
+    lhs = lhs.astype(BF16)
+    row_octant = lax.rem(lax.broadcasted_iota(jnp.int32, (32, width), 0), 8)
+
+    def lift(o, total):
+        out = jnp.dot(lhs, up_ref[o], preferred_element_type=F32)
+        return total + jnp.where(row_octant == o, out, 0.0)
+
+    lifted = lax.fori_loop(0, 8, lift, jnp.zeros((32, width), F32), unroll=True)
+    lifted = jnp.sum(lifted, axis=0, keepdims=True)
+    share[0:1, :] = lifted[:, :LANES]
+    share[1:2, :] = lifted[:, LANES:]
+
+
+def pack(cell_ids, leaf_ids, own, body, upward_ops, ranks):
+    width = own.shape[1]
+    cap = cell_ids.shape[0] // ranks
+    rows = 4 * (leaf_ids.shape[0] // ranks)
+    smem = pl.BlockSpec(memory_space=pltpu.SMEM)
+    vmem = pl.BlockSpec(memory_space=pltpu.VMEM)
+    return pl.pallas_call(
+        pack_kernel,
+        out_shape=(
+            jax.ShapeDtypeStruct((ranks, cap, width), BF16),
+            jax.ShapeDtypeStruct((ranks, rows, LANES), F32),
+            jax.ShapeDtypeStruct((2, LANES), F32),
+        ),
+        in_specs=[smem] * 2 + [vmem] * 3,
+        out_specs=(vmem,) * 3,
+        scratch_shapes=[
+            pltpu.VMEM((2 * own.shape[0], LANES), F32),
+            pltpu.VMEM((ranks * 2 * cap, LANES), F32),
+        ],
+        compiler_params=pltpu.CompilerParams(vmem_limit_bytes=32 * 1024 * 1024),
+    )(cell_ids, leaf_ids, own, body, upward_ops)
+
+
+def exchange_kernel(
+    weight_ref,
+    share,
+    down_ref,
+    out_cells,
+    out_body,
+    got_cells,
+    got_body,
+    far_ref,
+    shares,
+    send_sems,
+    recv_sems,
+    local_sems,
+):
+    me = lax.axis_index(AXES)
+    ranks = shares.shape[0]
+    tops = ranks // 2
+    width = 2 * LANES
+    barrier = pltpu.get_barrier_semaphore()
+
+    def greet(d, carry):
+        pl.semaphore_signal(
+            barrier,
+            inc=1,
+            device_id=partner(lax.rem(me + d, ranks)),
+            device_id_type=pl.DeviceIdType.MESH,
+        )
+        return carry
+
+    lax.fori_loop(1, ranks, greet, 0)
+    keep = [
+        pltpu.make_async_copy(out_cells.at[me], got_cells.at[me], local_sems.at[0]),
+        pltpu.make_async_copy(out_body.at[me], got_body.at[me], local_sems.at[1]),
+    ]
+    for copy in keep:
+        copy.start()
+    shares[me] = share[...]
+    pl.semaphore_wait(barrier, ranks - 1)
+
+    def remote(src, dst, k, r):
+        return pltpu.make_async_remote_copy(
+            src_ref=src,
+            dst_ref=dst,
+            send_sem=send_sems.at[k],
+            recv_sem=recv_sems.at[k],
+            device_id=partner(r),
+            device_id_type=pl.DeviceIdType.MESH,
+        )
+
+    def send(d, carry):
+        r = lax.rem(me + d, ranks)
+        remote(share, shares.at[me], 2, r).start()
+        remote(out_cells.at[r], got_cells.at[me], 0, r).start()
+        remote(out_body.at[r], got_body.at[me], 1, r).start()
+        return carry
+
+    lax.fori_loop(1, ranks, send, 0)
+
+    whole = pl.ds(0, ranks - 1)
+    later = lax.rem(me + 1, ranks)
+    remote(shares.at[whole], shares.at[whole], 2, later).wait_recv()
+
+    top = me // 2
+
+    def weigh(t, total):
+        pair = shares[2 * t] + shares[2 * t + 1]
+        return total + weight_ref[top * tops + t] * pair
+
+    coarse = lax.fori_loop(0, tops, weigh, jnp.zeros((2, LANES), F32))
+    coarse = jnp.concatenate([coarse[0:1, :], coarse[1:2, :]], 1)
+    coarse = jnp.broadcast_to(coarse, (16, width)).astype(BF16)
+    for o in range(8):
+        out = jnp.dot(coarse, down_ref[o], preferred_element_type=F32)
+        far_ref[o : o + 1, :] = out[0:1, :]
+
+    for copy in keep:
+        copy.wait()
+    remote(shares.at[whole], shares.at[whole], 2, later).wait_send()
+    remote(out_cells.at[whole], got_cells.at[whole], 0, later).wait()
+    remote(out_body.at[whole], got_body.at[whole], 1, later).wait()
+
+
+def exchange(weight, share, downward_ops, out_cells, out_body):
+    ranks, _, width = out_cells.shape
+    smem = pl.BlockSpec(memory_space=pltpu.SMEM)
+    vmem = pl.BlockSpec(memory_space=pltpu.VMEM)
+    hbm = pl.BlockSpec(memory_space=pl.ANY)
+    return pl.pallas_call(
+        exchange_kernel,
+        out_shape=(
+            jax.ShapeDtypeStruct(out_cells.shape, BF16),
+            jax.ShapeDtypeStruct(out_body.shape, F32),
+            jax.ShapeDtypeStruct((8, width), F32),
+        ),
+        in_specs=[smem, vmem, vmem, hbm, hbm],
+        out_specs=(hbm, hbm, vmem),
+        scratch_shapes=[
+            pltpu.VMEM((ranks, 2, LANES), F32),
+            pltpu.SemaphoreType.DMA((3,)),
+            pltpu.SemaphoreType.DMA((3,)),
+            pltpu.SemaphoreType.DMA((2,)),
+        ],
+        compiler_params=pltpu.CompilerParams(
+            collective_id=0,
+            has_side_effects=True,
+            vmem_limit_bytes=32 * 1024 * 1024,
+        ),
+    )(weight, share, downward_ops, out_cells, out_body)
+
+
 def main_kernel(
-    src_ref,
-    near_ref,
+    src_hbm,
+    near_hbm,
     op_ref,
     own_ref,
     got_ref,
@@ -52,32 +243,28 @@
     group_lo,
     group_hi,
     tr_ref,
-    tr_sem,
+    src_ref,
+    near_ref,
+    sems,
     *picked,
     list_width,
     op_count,
     pitch,
 ):
     cells = own_ref.shape[0]
-    near_count = near_ref.shape[1]
+    near_count = near_hbm.shape[0] // cells
     list_pad = op_ref.shape[1]
-    tr_copy = pltpu.make_async_copy(tr_hbm, tr_ref, tr_sem)
+    src_copy = pltpu.make_async_copy(src_hbm, src_ref, sems.at[0])
+    near_copy = pltpu.make_async_copy(near_hbm, near_ref, sems.at[1])
+    tr_copy = pltpu.make_async_copy(tr_hbm, tr_ref, sems.at[2])
+    near_copy.start()
+    src_copy.start()
     tr_copy.start()
     for buf in picked:
         buf[...] = jnp.zeros_like(buf)
 
-    def spread(ref, base):
-        def step(i, carry):
-            rows = ref[pl.ds(pl.multiple_of(i * 16, 16), 16), :].astype(F32)
-            at = base + i * 32
-            tab[pl.ds(at, 16, stride=2), :] = rows[:, :LANES]
-            tab[pl.ds(at + 1, 16, stride=2), :] = rows[:, LANES:]
-            return carry
-
-        lax.fori_loop(0, ref.shape[0] // 16, step, 0)
-
-    spread(own_ref, 0)
-    spread(got_ref, 2 * cells)
+    halves_in_rows(own_ref, tab, 0)
+    halves_in_rows(got_ref, tab, 2 * cells)
 
     group_lo[...] = jnp.zeros_like(group_lo)
     group_hi[...] = jnp.zeros_like(group_hi)
@@ -85,7 +272,8 @@
     def features(ref, first, stage, is_target):
         def step(i, carry):
             at = pl.multiple_of(i * 8, 8)
-            axes = [pieces(ref[a, pl.ds(at, 8), :] - 0.5, 2) for a in range(3)]
+            block = [ref[pl.ds(at * 4 + a, 8, stride=4), :] for a in range(4)]
+            axes = [pieces(b - 0.5, 2) for b in block[:3]]
             norm = jnp.zeros((8, LANES), F32)
             for high, low in axes:
                 norm = norm + (high + low) * (high + low)
@@ -97,27 +285,29 @@
                 rows = twice[0] * 2 + twice[1] * 2 + pieces(norm, 3) + [one] * 3
             else:
                 rows = (highs + lows) * 2 + [one] * 3 + pieces(norm + SOFTENING, 3)
-                charge[pl.ds(first + at, 8), :] = ref[3, pl.ds(at, 8), :]
+                charge[pl.ds(first + at, 8), :] = block[3]
             for k, row in enumerate(rows):
                 stage[pl.ds(at * FEAT + k, 8, stride=FEAT), :] = row
             return carry
 
-        lax.fori_loop(0, ref.shape[1] // 8, step, 0)
+        lax.fori_loop(0, ref.shape[0] // 32, step, 0, unroll=4)
 
     def packed(stage, out, first, count):
         def step(i, carry):
             out[first + i] = stage[pl.ds(pl.multiple_of(i * FEAT, FEAT), FEAT), :].astype(BF16)
             return carry
 
-        lax.fori_loop(0, count, step, 0)
+        lax.fori_loop(0, count, step, 0, unroll=8)
 
     features(ownp_ref, 0, group_lo, True)
     packed(group_lo, target, 0, cells)
     features(ownp_ref, 0, group_hi, False)
     packed(group_hi, source, 0, cells)
     features(gotp_ref, cells, group_lo, False)
-    packed(group_lo, source, cells, gotp_ref.shape[1])
-
+    packed(group_lo, source, cells, gotp_ref.shape[0] // 4)
+
+    near_copy.wait()
+    src_copy.wait()
     op_ids = lax.broadcasted_iota(jnp.int32, (op_count, list_pad), 0)
 
     def group(cell, buf):
@@ -138,14 +328,16 @@
         for u in range(UNROLL):
             cell = c * UNROLL + u
             x = target[cell]
+            src_at = cell * list_width
+            near_at = cell * near_count
             total = jnp.zeros((LANES, LANES), F32)
             taken = 0
             for p in range(0, near_count, 2):
                 for j in range(taken, min(taken + per_pair, list_width)):
-                    row = pl.multiple_of(src_ref[cell, j], 2)
+                    row = pl.multiple_of(src_ref[src_at + j], 2)
                     picked[u][2 * j : 2 * j + 2, :] = tab[pl.ds(row, 2), :]
                 taken += per_pair
-                ids = [near_ref[cell, n] for n in range(p, min(p + 2, near_count))]
+                ids = [near_ref[near_at + n] for n in range(p, min(p + 2, near_count))]
                 y = [source[i] for i in ids]
                 y = jnp.concatenate(y, axis=1) if len(y) > 1 else y[0]
                 dist = lax.dot_general(
@@ -186,12 +378,12 @@
 
 def main_call(src, near, ops, own, got, own_p, got_p, far, translate_ops):
     cells = own.shape[0]
-    list_width = src.shape[1]
+    list_width = src.shape[0] // cells
     list_pad = ops.shape[1]
     op_count = translate_ops.shape[0]
-    tables = cells + got_p.shape[1]
+    tables = cells + got_p.shape[0] // 4
     pitch = cells + 8
-    smem = pl.BlockSpec(memory_space=pltpu.SMEM)
+    hbm = pl.BlockSpec(memory_space=pl.ANY)
     vmem = pl.BlockSpec(memory_space=pltpu.VMEM)
     return pl.pallas_call(
         functools.partial(
@@ -201,7 +393,7 @@
             jax.ShapeDtypeStruct((cells, 2 * LANES), F32),
             jax.ShapeDtypeStruct((cells, LANES), F32),
         ),
-        in_specs=[smem, smem] + [vmem] * 6 + [pl.BlockSpec(memory_space=pl.ANY)],
+        in_specs=[hbm, hbm] + [vmem] * 6 + [hbm],
         out_specs=(vmem, vmem),
         scratch_shapes=[
             pltpu.VMEM((2 * (cells + got.shape[0]), LANES), F32),
@@ -211,7 +403,9 @@
             pltpu.VMEM((op_count * pitch, LANES), F32),
             pltpu.VMEM((op_count * pitch, LANES), F32),
             pltpu.VMEM(translate_ops.shape, BF16),
-            pltpu.SemaphoreType.DMA,
+            pltpu.SMEM(src.shape, jnp.int32),
+            pltpu.SMEM(near.shape, jnp.int32),
+            pltpu.SemaphoreType.DMA((3,)),
         ]
         + [pltpu.VMEM((2 * list_pad, LANES), F32)] * UNROLL,
         compiler_params=pltpu.CompilerParams(vmem_limit_bytes=60 * 1024 * 1024),
@@ -233,45 +427,23 @@
     near_leaves,
     move_counts,
 ):
-    highest = lax.Precision.HIGHEST
     cells, width = multipole.shape
     leaf_size = positions.shape[2]
     ranks = lax.axis_size(AXES)
-    rank = lax.axis_index(AXES)
-    tops = top_weight.shape[0]
-
-    octants = jnp.sum(multipole.astype(F32).reshape(cells // 8, 8, width), axis=0)
-    share = jnp.dot(
-        octants.reshape(1, 8 * width),
-        upward_ops.astype(F32).reshape(8 * width, width),
-        precision=highest,
-        preferred_element_type=F32,
+
+    body = jnp.concatenate([positions, charges[:, None, :]], 1)
+    flat = body.reshape(-1, leaf_size)
+    out_cells, out_body, share = pack(
+        (send_cells * 2).reshape(-1),
+        (send_leaves * 4).reshape(-1),
+        multipole,
+        flat,
+        upward_ops,
+        ranks,
     )
-
-    body = jnp.concatenate([positions, charges[:, None, :]], 1)
-    sent = body[send_leaves].reshape(ranks, -1, leaf_size)
-    share_rows = jnp.broadcast_to(share.reshape(1, 2, leaf_size), (ranks, 2, leaf_size))
-    sent = jnp.concatenate([sent, share_rows], 1)
-    got = lax.all_to_all(sent, AXES, split_axis=0, concat_axis=0, tiled=True)
-
-    pick = (send_cells.reshape(-1, 1) == jnp.arange(cells, dtype=jnp.int32)[None, :])
-    out_cells = jnp.dot(pick.astype(BF16), multipole, preferred_element_type=F32)
-    out_cells = out_cells.astype(BF16).reshape(ranks, -1, width)
-    got_cells = lax.all_to_all(out_cells, AXES, split_axis=0, concat_axis=0, tiled=True)
-
-    shares = got[:, -2:, :].reshape(tops, ranks // tops, width)
-    top_sums = jnp.sum(shares, axis=1)
-    top = rank * tops // ranks
-    weight = lax.dynamic_slice_in_dim(top_weight, top, 1, 0)
-    coarse = jnp.dot(weight, top_sums, precision=highest, preferred_element_type=F32)
-    coarse = jnp.broadcast_to(coarse.astype(BF16)[None], (8, 1, width))
-    far = lax.dot_general(
-        coarse, downward_ops, (((2,), (1,)), ((0,), (0,))), preferred_element_type=F32
-    ).reshape(8, width)
-
-    own_p = jnp.transpose(body, (1, 0, 2))
-    got_p = got[:, :-2, :].reshape(-1, 4, leaf_size)
-    got_p = jnp.transpose(got_p, (1, 0, 2))
+    got_cells, got_body, far = exchange(
+        top_weight.reshape(-1), share, downward_ops, out_cells, out_body
+    )
     list_pad = -(-list_operator.shape[1] // 64) * 64
     ops = jnp.pad(
         list_operator,
@@ -279,13 +451,13 @@
         constant_values=translate_ops.shape[0],
     )
     local_exp, potential = main_call(
-        list_source * 2,
-        near_leaves,
+        (list_source * 2).reshape(-1),
+        near_leaves.reshape(-1),
         ops,
         multipole,
         got_cells.reshape(-1, width),
-        own_p,
-        got_p,
+        flat,
+        got_body.reshape(-1, leaf_size),
         far,
         translate_ops,
     )

time: 222 us -> 196 us (0.88)
  waiting for transfers between devices: 33.1 us -> 1.45 us
  Pallas kernels: 141 us -> 163 us
  starting transfers between devices: 26.6 us -> 9.76 us
  local copies, waits for them, and re-layouts: 8.86 us -> 13.5 us
  matrix products: 4.34 us -> 0 us
    pallas_call x0 -> x2, Pallas kernels: none -> 46.6 us  [the longest x1 42.9 us: exchange(): pl.pallas_call(exchange_kernel, out_shape=(jax.ShapeDtypeStruct(out_cells...]
    all_to_all x2 -> x0, waiting for transfers between devices: 31.7 us -> none  [the longest x1 18.8 us: per_device(): got = lax.all_to_all(sent, AXES, split_axis=0, concat_axis=0, tiled=True)]
    pallas_call x1, Pallas kernels: 141 us -> 117 us  [main_call(): pl.pallas_call(functools.partial(main_kernel, list_width=list_width, op_c...]
    all_to_all x2 -> x0, starting transfers between devices: 16.9 us -> none  [the longest x1 10.4 us: per_device(): got = lax.all_to_all(sent, AXES, split_axis=0, concat_axis=0, tiled=True)]
    unnamed x22 -> x18, local copies, waits for them, and re-layouts: 2.1 us -> 7.85 us
    dot_general x4 -> x0, matrix products: 4.34 us -> none  [the longest x1 1.74 us: per_device(): jnp.dot(octants.reshape(1, 8 * width), upward_ops.astype(F32).reshape(8 *...]
  transfers between devices with their start and end apart: 4 -> 2, of which waited for: 3 -> 1; matrix products, arithmetic and copies ran while one was open for 5% -> 0% of each run, Pallas kernels for 0% -> 0%
where the time goes in v2:
time: 196 us; the launch traced here: 195 us
  Pallas kernels  163 us (83%)
  local copies, waits for them, and re-layouts  13.5 us (7%)
  starting transfers between devices  9.76 us (5%)
  other arithmetic  6.25 us (3%)
    pallas_call x1, Pallas kernels, main_call(): pl.pallas_call(functools.partial(main_kernel, list_width=list_width, op_c...  117 us
    pallas_call x1, Pallas kernels, exchange(): pl.pallas_call(exchange_kernel, out_shape=(jax.ShapeDtypeStruct(out_cells...  42.9 us
    ppermute x2, starting transfers between devices, shifted(): return lax.ppermute(x, axis, pairs)  9.76 us
    unnamed x18, local copies, waits for them, and re-layouts  7.85 us
  transfers between devices with their start and end apart: 2, of which 1 were waited for; matrix products, arithmetic and copies ran while one was open for 0% of the time, Pallas kernels for 0%

profile of v2, /device:TPU:8, one launch (start us, length us, event | category | flops | bytes accessed | tf_op | source)
XLA Modules:
  0.0 194.9 jit_solution(10275102192882270447)
XLA Ops:
  0.6 1.1 pad_maximum_fusion
  1.7 0.7 fusion
  2.5 0.3 copy.23
  2.8 0.0 copy-start
  2.8 0.7 broadcast_multiply_fusion.1
  3.6 0.1 copy.21
  3.7 0.1 reshape.41.cell_ids
  3.7 0.7 broadcast_multiply_fusion.2
  4.4 0.1 copy.22
  4.6 0.1 reshape.42.leaf_ids
  4.7 0.8 reshape.40.weight_ref
  5.5 0.9 broadcast_multiply_fusion
  6.4 0.1 copy.18
  6.6 1.0 reshape.38.src_hbm
  7.6 1.1 copy.20
  8.7 0.9 copy.19
  9.5 0.8 reshape.39.near_hbm
  10.3 0.7 pad.4.op_ref
  11.1 0.0 copy-start.7
  11.1 0.0 copy-start.1
  11.1 1.2 copy-done.1
  12.3 0.0 copy-start.5
  12.3 0.9 copy-done.5
  13.2 3.7 %shard_map.148 = (bf16[128,16,256]{2,1,0:T(8,128)(2,1)S(1)}, f32[128,16,128]{2,1,0:T(8,128)S(1)}, f32[2,128]{1,0:T(2,128)S(1)}) custom-call(s32[2048]{0:T(1024)S(1)} %reshape.41.cell_ids, s32[512]{0:T(512)S(1)} %reshape.42.leaf_ids, bf16[256,256]{1,0:T(8,128)(2,1)S(1)} %copy-done.5, f32[1024,128]{1,0:T(8,128)S(1)} %bitcast.10, bf16[8,256,256]{2,1,0:T(8,128)(2,1)S(1)} %copy-done.1), custom_call_target="tpu_custom_call" | custom-call | tf_op jit(solution)/shard_map/pallas_call | solution.py:100
  16.9 0.0 copy-start.2
  16.9 1.2 copy-done.2
  18.1 42.9 %shard_map.149 = (bf16[128,16,256]{2,1,0:T(8,128)(2,1)S(1)}, f32[128,16,128]{2,1,0:T(8,128)S(1)}, f32[8,256]{1,0:T(8,128)S(1)}) custom-call(f32[4096]{0:T(1024)S(1)} %reshape.40.weight_ref, f32[2,128]{1,0:T(2,128)S(1)} %get-tuple-element.11.share, bf16[8,256,256]{2,1,0:T(8,128)(2,1)S(1)} %copy-done.2, bf16[128,16,256]{2,1,0:T(8,128)(2,1)S(1)} %get-tuple-element.12.out_cells, ...), custom_call_target="tpu_custom_call" | custom-call | tf_op jit(solution)/shard_map/pallas_call | solution.py:204
  61.0 0.0 copy-start.3
  61.0 1.0 copy-done.3
  62.0 0.0 copy-start.4
  62.0 1.0 copy-done.4
  63.0 0.0 copy-start.6
  63.0 0.6 copy-done.6
  63.6 0.0 copy-done
  63.6 116.6 %shard_map.150 = (f32[256,256]{1,0:T(8,128)}, f32[256,128]{1,0:T(8,128)}) custom-call(s32[48384]{0:T(1024)} %reshape.38.src_hbm, s32[6912]{0:T(1024)} %reshape.39.near_hbm, s32[256,192]{1,0:T(8,128)} %pad.4.op_ref, bf16[256,256]{1,0:T(8,128)(2,1)} %own_ref.3, bf16[2048,256]{1,0:T(8,128)(2,1)} %bitcast.12, f32[1024,128]{1,0:T(8,128)} %bitcast.11, ...), custom_call_target="tpu_custom_call" | custom-call | tf_op jit(solution)/shard_map/pallas_call | solution.py:388
  180.2 0.7 slice_bitcast_fusion.1
  180.9 0.0 copy-done.7
  180.9 0.6 fusion.2
  181.6 0.6 iota_compare_fusion
  182.2 0.1 broadcast_select_fusion
  182.3 2.2 %collective-permute-start.1 = (f32[8,5,128]{2,0,1:T(8,128)S(1)}, f32[8,5,128]{2,0,1:T(8,128)S(1)}, u32[]{:S(2)}, u32[]{:S(2)}) collective-permute-start(f32[8,5,128]{2,0,1:T(8,128)S(1)} %broadcast_select_fusion), channel_id=1, source_target_pairs={{0,1},{1,2},{2,3},{3,4},{4,5},{5,6},{6,7},{7,8},{8,9},{9,10},{10,1... | collective-permute-start | bytes 61448 | tf_op jit(solution)/shard_map/ppermute | solution.py:24
  184.5 0.7 iota_compare_fusion.1
  185.2 0.1 maximum_select_fusion
  185.2 7.5 %collective-permute-start = (f32[8,5,128]{2,0,1:T(8,128)S(1)}, f32[8,5,128]{2,0,1:T(8,128)S(1)}, u32[]{:S(2)}, u32[]{:S(2)}) collective-permute-start(f32[8,5,128]{2,0,1:T(8,128)S(1)} %maximum_select_fusion), channel_id=1, source_target_pairs={{1,0},{2,1},{3,2},{4,3},{5,4},{6,5},{7,6},{8,7},{9,8},{10,9},{11,1... | collective-permute-start | bytes 61448 | tf_op jit(solution)/shard_map/ppermute | solution.py:24
  192.8 0.0 collective-permute-done.1
  192.8 1.4 collective-permute-done
  194.2 0.6 pad_maximum_fusion.1
  (2 shorter events, 0.0 us)
Async XLA Ops:
  2.8 60.8 %copy-start = (f32[256,4,128]{2,1,0:T(4,128)}, f32[256,4,128]{2,1,0:T(4,128)S(1)}, u32[]{:S(2)}) copy-start(f32[256,4,128]{2,1,0:T(4,128)S(1)} %copy.23) | copy-start | bytes 1572868
  11.1 169.9 %copy-start.7 = (s32[1,2]{1,0:T(1,128)S(1)}, s32[1,2]{1,0:T(1,128)}, u32[]{:S(2)}) copy-start(s32[1,2]{1,0:T(1,128)} %param.25) | copy-start | bytes 28
  11.1 1.2 copy-start.1
  12.3 0.9 copy-start.5
  16.9 1.2 copy-start.2
  61.0 1.0 copy-start.3
  62.0 1.0 copy-start.4
  63.0 0.6 copy-start.6
  182.3 10.5 %collective-permute-start.1 = (f32[8,5,128]{2,0,1:T(8,128)S(1)}, f32[8,5,128]{2,0,1:T(8,128)S(1)}, u32[]{:S(2)}, u32[]{:S(2)}) collective-permute-start(f32[8,5,128]{2,0,1:T(8,128)S(1)} %broadcast_select_fusion), channel_id=1, source_target_pairs={{0,1},{1,2},{2,3},{3,4},{4,5},{5,6},{6,7},{7,8},{8,9},{9,10},{10,1... | collective-permute-start | bytes 61448 | tf_op jit(solution)/shard_map/ppermute | solution.py:24
  185.2 9.0 %collective-permute-start = (f32[8,5,128]{2,0,1:T(8,128)S(1)}, f32[8,5,128]{2,0,1:T(8,128)S(1)}, u32[]{:S(2)}, u32[]{:S(2)}) collective-permute-start(f32[8,5,128]{2,0,1:T(8,128)S(1)} %maximum_select_fusion), channel_id=1, source_target_pairs={{1,0},{2,1},{3,2},{4,3},{5,4},{6,5},{7,6},{8,7},{9,8},{10,9},{11,1... | collective-permute-start | bytes 61448 | tf_op jit(solution)/shard_map/ppermute | solution.py:24

commit v3 on v2

--- a/solution.py
+++ b/solution.py
@@ -14,8 +14,9 @@
 AXES = ("leaf", "sub")
 LANES = 128
 FEAT = 32
-UNROLL = 8
+UNROLL = 16
 KSTEP = 8
+SPREAD = 45
 
 
 def shifted(x, axis, by):
@@ -163,8 +164,8 @@
             device_id_type=pl.DeviceIdType.MESH,
         )
 
-    def send(d, carry):
-        r = lax.rem(me + d, ranks)
+    def send(k, carry):
+        r = lax.rem(me + lax.rem(k * SPREAD, ranks), ranks)
         remote(share, shares.at[me], 2, r).start()
         remote(out_cells.at[r], got_cells.at[me], 0, r).start()
         remote(out_body.at[r], got_body.at[me], 1, r).start()
@@ -233,9 +234,12 @@
     ownp_ref,
     gotp_ref,
     far_ref,
+    moves_ref,
     tr_hbm,
     local_ref,
     pot_ref,
+    lower_ref,
+    upper_ref,
     tab,
     charge,
     target,
@@ -357,6 +361,14 @@
     lax.fori_loop(0, cells // UNROLL, leaves, 0)
     group(cells - 1, picked[UNROLL - 1])
 
+    for out, column in ((lower_ref, 0), (upper_ref, 1)):
+        for s in range(MCAP):
+            leaf = s if column == 0 else cells - 1 - s
+            kept = s < moves_ref[0, column]
+            block = ownp_ref[4 * leaf : 4 * leaf + 4, :]
+            out[s, 0:4, :] = jnp.where(kept, block, 0.0)
+            out[s, 4:5, :] = jnp.where(kept, pot_ref[leaf : leaf + 1, :], 0.0)
+
     tr_copy.wait()
     far = jnp.concatenate([far_ref[...]] * (cells // 8), 0)
     local_ref[...] = far
@@ -376,7 +388,7 @@
     lax.fori_loop(0, op_count // KSTEP, translate, 0)
 
 
-def main_call(src, near, ops, own, got, own_p, got_p, far, translate_ops):
+def main_call(src, near, ops, own, got, own_p, got_p, far, moves, translate_ops):
     cells = own.shape[0]
     list_width = src.shape[0] // cells
     list_pad = ops.shape[1]
@@ -392,9 +404,11 @@
         out_shape=(
             jax.ShapeDtypeStruct((cells, 2 * LANES), F32),
             jax.ShapeDtypeStruct((cells, LANES), F32),
+            jax.ShapeDtypeStruct((MCAP, 5, LANES), F32),
+            jax.ShapeDtypeStruct((MCAP, 5, LANES), F32),
         ),
-        in_specs=[hbm, hbm] + [vmem] * 6 + [hbm],
-        out_specs=(vmem, vmem),
+        in_specs=[hbm, hbm] + [vmem] * 6 + [pl.BlockSpec(memory_space=pltpu.SMEM), hbm],
+        out_specs=(vmem,) * 4,
         scratch_shapes=[
             pltpu.VMEM((2 * (cells + got.shape[0]), LANES), F32),
             pltpu.VMEM((tables, LANES), F32),
@@ -409,7 +423,7 @@
         ]
         + [pltpu.VMEM((2 * list_pad, LANES), F32)] * UNROLL,
         compiler_params=pltpu.CompilerParams(vmem_limit_bytes=60 * 1024 * 1024),
-    )(src, near, ops, own, got, own_p, got_p, far, translate_ops)
+    )(src, near, ops, own, got, own_p, got_p, far, moves, translate_ops)
 
 
 def per_device(
@@ -450,7 +464,7 @@
         ((0, 0), (0, list_pad - list_operator.shape[1])),
         constant_values=translate_ops.shape[0],
     )
-    local_exp, potential = main_call(
+    local_exp, potential, lower, upper = main_call(
         (list_source * 2).reshape(-1),
         near_leaves.reshape(-1),
         ops,
@@ -459,16 +473,10 @@
         flat,
         got_body.reshape(-1, leaf_size),
         far,
+        move_counts,
         translate_ops,
     )
 
-    def payload(a, b):
-        return jnp.concatenate([body[a:b], potential[a:b, None, :]], 1)
-
-    slot = jnp.arange(MCAP, dtype=jnp.int32)
-    lower = jnp.where((slot < move_counts[0, 0])[:, None, None], payload(0, MCAP), 0.0)
-    upper = payload(cells - MCAP, cells)[::-1]
-    upper = jnp.where((slot < move_counts[0, 1])[:, None, None], upper, 0.0)
     from_upper = shifted(lower, AXES, -1)
     from_lower = shifted(upper, AXES, 1)
     arrivals = jnp.concatenate([from_upper, from_lower], 0)

time: 196 us -> 186 us (0.949)
  Pallas kernels: 163 us -> 154 us
  waiting for transfers between devices: 1.45 us -> 7.73 us
  other arithmetic: 6.25 us -> 3.47 us
  starting transfers between devices: 9.76 us -> 7.13 us
    ppermute x2, waiting for transfers between devices: 1.45 us -> 7.73 us  [shifted(): return lax.ppermute(x, axis, pairs)]
    pallas_call x1, Pallas kernels: 117 us -> 112 us  [main_call(): pl.pallas_call(functools.partial(main_kernel, list_width=list_width, op_c...]
    pallas_call x1, Pallas kernels: 42.9 us -> 38.4 us  [exchange(): pl.pallas_call(exchange_kernel, out_shape=(jax.ShapeDtypeStruct(out_cells...]
    ppermute x2, starting transfers between devices: 9.76 us -> 7.13 us  [shifted(): return lax.ppermute(x, axis, pairs)]
    unnamed x18 -> x17, local copies, waits for them, and re-layouts: 7.85 us -> 8.45 us
where the time goes in v3:
time: 186 us
  Pallas kernels  154 us (83%)
  local copies, waits for them, and re-layouts  12.7 us (7%)
  waiting for transfers between devices  7.73 us (4%)
  starting transfers between devices  7.13 us (4%)
  other arithmetic  3.47 us (2%)
    pallas_call x1, Pallas kernels, main_call(): pl.pallas_call(functools.partial(main_kernel, list_width=list_width, op_c...  112 us
    pallas_call x1, Pallas kernels, exchange(): pl.pallas_call(exchange_kernel, out_shape=(jax.ShapeDtypeStruct(out_cells...  38.4 us
    unnamed x17, local copies, waits for them, and re-layouts  8.45 us
    ppermute x2, waiting for transfers between devices, shifted(): return lax.ppermute(x, axis, pairs)  7.73 us
    ppermute x2, starting transfers between devices, shifted(): return lax.ppermute(x, axis, pairs)  7.13 us
  transfers between devices with their start and end apart: 2, of which 1 were waited for; matrix products, arithmetic and copies ran while one was open for 0% of the time, Pallas kernels for 0%

profile of v3, /device:TPU:8, one launch (start us, length us, event | category | flops | bytes accessed | tf_op | source)
XLA Modules:
  0.0 185.7 jit_solution(705132978196918238)
XLA Ops:
  0.6 1.1 pad_maximum_fusion
  1.7 0.3 copy.24
  2.1 0.0 copy-start
  2.1 0.7 broadcast_multiply_fusion.1
  2.8 0.1 copy.22
  2.9 0.1 reshape.33.cell_ids
  3.0 0.7 broadcast_multiply_fusion.2
  3.7 0.1 copy.23
  3.8 0.1 reshape.34.leaf_ids
  3.9 0.8 reshape.32.weight_ref
  4.8 0.9 broadcast_multiply_fusion
  5.7 0.1 copy.19
  5.8 1.0 reshape.30.src_hbm
  6.9 1.1 copy.21
  7.9 0.9 copy.20
  8.8 0.8 reshape.31.near_hbm
  9.6 0.7 pad.4.op_ref
  10.3 0.0 copy-start.1
  10.3 1.2 copy-done.1
  11.5 0.0 copy-start.5
  11.5 0.9 copy-done.5
  12.4 3.7 %shard_map.148 = (bf16[128,16,256]{2,1,0:T(8,128)(2,1)S(1)}, f32[128,16,128]{2,1,0:T(8,128)S(1)}, f32[2,128]{1,0:T(2,128)S(1)}) custom-call(s32[2048]{0:T(1024)S(1)} %reshape.33.cell_ids, s32[512]{0:T(512)S(1)} %reshape.34.leaf_ids, bf16[256,256]{1,0:T(8,128)(2,1)S(1)} %copy-done.5, f32[1024,128]{1,0:T(8,128)S(1)} %bitcast.4, bf16[8,256,256]{2,1,0:T(8,128)(2,1)S(1)} %copy-done.1), custom_call_target="tpu_custom_call" | custom-call | tf_op jit(solution)/shard_map/pallas_call | solution.py:101
  16.1 0.0 copy-start.2
  16.2 1.2 copy-done.2
  17.4 38.4 %shard_map.149 = (bf16[128,16,256]{2,1,0:T(8,128)(2,1)S(1)}, f32[128,16,128]{2,1,0:T(8,128)S(1)}, f32[8,256]{1,0:T(8,128)S(1)}) custom-call(f32[4096]{0:T(1024)S(1)} %reshape.32.weight_ref, f32[2,128]{1,0:T(2,128)S(1)} %get-tuple-element.13.share, bf16[8,256,256]{2,1,0:T(8,128)(2,1)S(1)} %copy-done.2, bf16[128,16,256]{2,1,0:T(8,128)(2,1)S(1)} %get-tuple-element.14.out_cells, ...), custom_call_target="tpu_custom_call" | custom-call | tf_op jit(solution)/shard_map/pallas_call | solution.py:205
  55.7 0.0 copy-start.3
  55.8 1.0 copy-done.3
  56.7 0.0 copy-start.4
  56.7 1.0 copy-done.4
  57.7 0.0 copy-start.6
  57.7 0.6 copy-done.6
  58.3 0.0 copy-done
  58.3 111.9 %shard_map.150 = (f32[256,256]{1,0:T(8,128)}, f32[256,128]{1,0:T(8,128)}, f32[8,5,128]{2,1,0:T(8,128)}, f32[8,5,128]{2,1,0:T(8,128)}) custom-call(s32[48384]{0:T(1024)} %reshape.30.src_hbm, s32[6912]{0:T(1024)} %reshape.31.near_hbm, s32[256,192]{1,0:T(8,128)} %pad.4.op_ref, bf16[256,256]{1,0:T(8,128)(2,1)} %own_ref.3, bf16[2048,256]{1,0:T(8,128)(2,1)} %bitcast.6, ...), custom_call_target="tpu_custom_call" | custom-call | tf_op jit(solution)/shard_map/pallas_call | solution.py:400
  170.2 5.2 %collective-permute-start = (f32[8,5,128]{2,1,0:T(8,128)}, f32[8,5,128]{2,1,0:T(8,128)S(1)}, u32[]{:S(2)}, u32[]{:S(2)}) collective-permute-start(f32[8,5,128]{2,1,0:T(8,128)} %get-tuple-element.21), channel_id=1, source_target_pairs={{1,0},{2,1},{3,2},{4,3},{5,4},{6,5},{7,6},{8,7},{9,8},{10,9},{11,1... | collective-permute-start | bytes 61448 | tf_op jit(solution)/shard_map/ppermute | solution.py:25
  175.4 1.9 %collective-permute-start.1 = (f32[8,5,128]{2,1,0:T(8,128)}, f32[8,5,128]{2,1,0:T(8,128)S(1)}, u32[]{:S(2)}, u32[]{:S(2)}) collective-permute-start(f32[8,5,128]{2,1,0:T(8,128)} %get-tuple-element.22), channel_id=1, source_target_pairs={{0,1},{1,2},{2,3},{3,4},{4,5},{5,6},{6,7},{7,8},{8,9},{9,10},{10,1... | collective-permute-start | bytes 61448 | tf_op jit(solution)/shard_map/ppermute | solution.py:25
  177.3 0.0 collective-permute-done
  177.3 7.7 %collective-permute-done.1 = f32[8,5,128]{2,1,0:T(8,128)S(1)} collective-permute-done((f32[8,5,128]{2,1,0:T(8,128)}, f32[8,5,128]{2,1,0:T(8,128)S(1)}, u32[]{:S(2)}, u32[]{:S(2)}) %collective-permute-start.1) | collective-permute-done | bytes 20512 | tf_op jit(solution)/shard_map/ppermute | solution.py:25
  185.1 0.6 copy.25
  (1 shorter events, 0.0 us)
Async XLA Ops:
  2.1 56.2 %copy-start = (f32[256,4,128]{2,1,0:T(4,128)}, f32[256,4,128]{2,1,0:T(4,128)S(1)}, u32[]{:S(2)}) copy-start(f32[256,4,128]{2,1,0:T(4,128)S(1)} %copy.24) | copy-start | bytes 1572868
  10.3 1.2 copy-start.1
  11.5 0.9 copy-start.5
  16.1 1.2 copy-start.2
  55.7 1.0 copy-start.3
  56.7 1.0 copy-start.4
  57.7 0.6 copy-start.6
  170.2 7.2 %collective-permute-start = (f32[8,5,128]{2,1,0:T(8,128)}, f32[8,5,128]{2,1,0:T(8,128)S(1)}, u32[]{:S(2)}, u32[]{:S(2)}) collective-permute-start(f32[8,5,128]{2,1,0:T(8,128)} %get-tuple-element.21), channel_id=1, source_target_pairs={{1,0},{2,1},{3,2},{4,3},{5,4},{6,5},{7,6},{8,7},{9,8},{10,9},{11,1... | collective-permute-start | bytes 61448 | tf_op jit(solution)/shard_map/ppermute | solution.py:25
  175.4 9.7 %collective-permute-start.1 = (f32[8,5,128]{2,1,0:T(8,128)}, f32[8,5,128]{2,1,0:T(8,128)S(1)}, u32[]{:S(2)}, u32[]{:S(2)}) collective-permute-start(f32[8,5,128]{2,1,0:T(8,128)} %get-tuple-element.22), channel_id=1, source_target_pairs={{0,1},{1,2},{2,3},{3,4},{4,5},{5,6},{6,7},{7,8},{8,9},{9,10},{10,1... | collective-permute-start | bytes 61448 | tf_op jit(solution)/shard_map/ppermute | solution.py:25

commit v4 on v3

--- a/solution.py
+++ b/solution.py
@@ -16,6 +16,7 @@
 FEAT = 32
 UNROLL = 16
 KSTEP = 8
+WINDOW = 8
 SPREAD = 45
 
 
@@ -247,7 +248,8 @@
     group_lo,
     group_hi,
     tr_ref,
-    src_ref,
+    window_a,
+    window_b,
     near_ref,
     sems,
     *picked,
@@ -258,11 +260,20 @@
     cells = own_ref.shape[0]
     near_count = near_hbm.shape[0] // cells
     list_pad = op_ref.shape[1]
-    src_copy = pltpu.make_async_copy(src_hbm, src_ref, sems.at[0])
+    windows = (window_a, window_b)
+    span = window_a.shape[0]
+
+    def fetch(slot, block):
+        at = pl.multiple_of(block * span, span)
+        return pltpu.make_async_copy(
+            src_hbm.at[pl.ds(at, span)], windows[slot], sems.at[3 * slot]
+        )
+
     near_copy = pltpu.make_async_copy(near_hbm, near_ref, sems.at[1])
     tr_copy = pltpu.make_async_copy(tr_hbm, tr_ref, sems.at[2])
     near_copy.start()
-    src_copy.start()
+    fetch(0, 0).start()
+    fetch(1, 1).start()
     tr_copy.start()
     for buf in picked:
         buf[...] = jnp.zeros_like(buf)
@@ -311,7 +322,6 @@
     packed(group_lo, source, cells, gotp_ref.shape[0] // 4)
 
     near_copy.wait()
-    src_copy.wait()
     op_ids = lax.broadcasted_iota(jnp.int32, (op_count, list_pad), 0)
 
     def group(cell, buf):
@@ -332,13 +342,16 @@
         for u in range(UNROLL):
             cell = c * UNROLL + u
             x = target[cell]
-            src_at = cell * list_width
+            slot = u // WINDOW
+            if u % WINDOW == 0:
+                fetch(slot, 2 * c + slot).wait()
+            src_at = (u % WINDOW) * list_width
             near_at = cell * near_count
             total = jnp.zeros((LANES, LANES), F32)
             taken = 0
             for p in range(0, near_count, 2):
                 for j in range(taken, min(taken + per_pair, list_width)):
-                    row = pl.multiple_of(src_ref[src_at + j], 2)
+                    row = pl.multiple_of(windows[slot][src_at + j], 2)
                     picked[u][2 * j : 2 * j + 2, :] = tab[pl.ds(row, 2), :]
                 taken += per_pair
                 ids = [near_ref[near_at + n] for n in range(p, min(p + 2, near_count))]
@@ -355,6 +368,12 @@
                 if p == 8 and pending is not None:
                     reduced(*pending)
             pending = (total, cell)
+            if u % WINDOW == WINDOW - 1:
+
+                @pl.when(c + 1 < cells // UNROLL)
+                def _():
+                    fetch(slot, 2 * (c + 1) + slot).start()
+
         reduced(*pending)
         return carry
 
@@ -388,9 +407,8 @@
     lax.fori_loop(0, op_count // KSTEP, translate, 0)
 
 
-def main_call(src, near, ops, own, got, own_p, got_p, far, moves, translate_ops):
+def main_call(list_width, src, near, ops, own, got, own_p, got_p, far, moves, translate_ops):
     cells = own.shape[0]
-    list_width = src.shape[0] // cells
     list_pad = ops.shape[1]
     op_count = translate_ops.shape[0]
     tables = cells + got_p.shape[0] // 4
@@ -417,9 +435,10 @@
             pltpu.VMEM((op_count * pitch, LANES), F32),
             pltpu.VMEM((op_count * pitch, LANES), F32),
             pltpu.VMEM(translate_ops.shape, BF16),
-            pltpu.SMEM(src.shape, jnp.int32),
+            pltpu.SMEM((src.shape[0] * WINDOW // cells,), jnp.int32),
+            pltpu.SMEM((src.shape[0] * WINDOW // cells,), jnp.int32),
             pltpu.SMEM(near.shape, jnp.int32),
-            pltpu.SemaphoreType.DMA((3,)),
+            pltpu.SemaphoreType.DMA((4,)),
         ]
         + [pltpu.VMEM((2 * list_pad, LANES), F32)] * UNROLL,
         compiler_params=pltpu.CompilerParams(vmem_limit_bytes=60 * 1024 * 1024),
@@ -464,8 +483,12 @@
         ((0, 0), (0, list_pad - list_operator.shape[1])),
         constant_values=translate_ops.shape[0],
     )
+    flat_lists = (list_source * 2).reshape(cells // WINDOW, -1)
+    span = -(-flat_lists.shape[1] // 1024) * 1024
+    flat_lists = jnp.pad(flat_lists, ((0, 0), (0, span - flat_lists.shape[1])))
     local_exp, potential, lower, upper = main_call(
-        (list_source * 2).reshape(-1),
+        list_source.shape[1],
+        flat_lists.reshape(-1),
         near_leaves.reshape(-1),
         ops,
         multipole,

time: 186 us -> 181 us (0.973)
  Pallas kernels: 154 us -> 150 us
    pallas_call x1, Pallas kernels: 112 us -> 108 us  [main_call(): pl.pallas_call(functools.partial(main_kernel, list_width=list_width, op_c...]
    unnamed x17 -> x19, local copies, waits for them, and re-layouts: 8.45 us -> 8.01 us
where the time goes in v4:
time: 181 us; the launch traced here: 180 us
  Pallas kernels  150 us (83%)
  local copies, waits for them, and re-layouts  11.4 us (6%)
  waiting for transfers between devices  7.73 us (4%)
  starting transfers between devices  7.12 us (4%)
  other arithmetic  3.54 us (2%)
    pallas_call x1, Pallas kernels, main_call(): pl.pallas_call(functools.partial(main_kernel, list_width=list_width, op_c...  108 us
    pallas_call x1, Pallas kernels, exchange(): pl.pallas_call(exchange_kernel, out_shape=(jax.ShapeDtypeStruct(out_cells...  38.4 us
    unnamed x19, local copies, waits for them, and re-layouts  8.01 us
    ppermute x2, waiting for transfers between devices, shifted(): return lax.ppermute(x, axis, pairs)  7.73 us
    ppermute x2, starting transfers between devices, shifted(): return lax.ppermute(x, axis, pairs)  7.12 us
    pallas_call x1, Pallas kernels, pack(): pl.pallas_call(pack_kernel, out_shape=(jax.ShapeDtypeStruct((ranks, cap,...  3.69 us
  transfers between devices with their start and end apart: 2, of which 1 were waited for; matrix products, arithmetic and copies ran while one was open for 0% of the time, Pallas kernels for 0%

profile of v4, /device:TPU:8, one launch (start us, length us, event | category | flops | bytes accessed | tf_op | source)
XLA Modules:
  0.0 180.3 jit_solution(18292689828837796730)
XLA Ops:
  0.6 0.0 copy-start.2
  0.6 1.2 pad_maximum_fusion
  1.8 0.3 copy.24
  2.2 0.0 copy-start
  2.2 0.7 broadcast_multiply_fusion.1
  2.9 0.1 copy.22
  3.0 0.1 reshape.37.cell_ids
  3.1 0.7 broadcast_multiply_fusion.2
  3.8 0.1 copy.23
  3.9 0.1 reshape.38.leaf_ids
  4.0 0.8 reshape.36.weight_ref
  4.8 0.9 broadcast_multiply_fusion
  5.8 0.1 copy.19
  5.9 0.2 reshape.33
  6.1 0.8 copy.26
  6.9 1.1 copy.21
  7.9 0.9 copy.20
  8.8 0.8 reshape.35.near_hbm
  9.6 0.7 pad.9.op_ref
  10.3 0.0 copy-start.1
  10.3 1.2 copy-done.1
  11.6 0.0 copy-start.5
  11.6 0.9 copy-done.5
  12.5 3.7 %shard_map.148 = (bf16[128,16,256]{2,1,0:T(8,128)(2,1)S(1)}, f32[128,16,128]{2,1,0:T(8,128)S(1)}, f32[2,128]{1,0:T(2,128)S(1)}) custom-call(s32[2048]{0:T(1024)S(1)} %reshape.37.cell_ids, s32[512]{0:T(512)S(1)} %reshape.38.leaf_ids, bf16[256,256]{1,0:T(8,128)(2,1)S(1)} %copy-done.5, f32[1024,128]{1,0:T(8,128)S(1)} %bitcast.7, bf16[8,256,256]{2,1,0:T(8,128)(2,1)S(1)} %copy-done.1), custom_call_target="tpu_custom_call" | custom-call | tf_op jit(solution)/shard_map/pallas_call | solution.py:102
  16.2 0.0 copy-done.2
  16.2 38.4 %shard_map.149 = (bf16[128,16,256]{2,1,0:T(8,128)(2,1)S(1)}, f32[128,16,128]{2,1,0:T(8,128)S(1)}, f32[8,256]{1,0:T(8,128)S(1)}) custom-call(f32[4096]{0:T(1024)S(1)} %reshape.36.weight_ref, f32[2,128]{1,0:T(2,128)S(1)} %get-tuple-element.13.share, bf16[8,256,256]{2,1,0:T(8,128)(2,1)S(1)} %copy-done.2, bf16[128,16,256]{2,1,0:T(8,128)(2,1)S(1)} %get-tuple-element.14.out_cells, ...), custom_call_target="tpu_custom_call" | custom-call | tf_op jit(solution)/shard_map/pallas_call | solution.py:206
  54.6 0.0 copy-start.3
  54.6 1.0 copy-done.3
  55.6 0.0 copy-start.4
  55.6 1.0 copy-done.4
  56.6 0.0 copy-start.6
  56.6 0.6 copy-done.6
  57.2 0.0 copy-done
  57.2 107.6 %shard_map.150 = (f32[256,256]{1,0:T(8,128)}, f32[256,128]{1,0:T(8,128)}, f32[8,5,128]{2,1,0:T(8,128)}, f32[8,5,128]{2,1,0:T(8,128)}) custom-call(s32[65536]{0:T(1024)} %bitcast.11, s32[6912]{0:T(1024)} %reshape.35.near_hbm, s32[256,192]{1,0:T(8,128)} %pad.9.op_ref, bf16[256,256]{1,0:T(8,128)(2,1)} %own_ref.3, bf16[2048,256]{1,0:T(8,128)(2,1)} %bitcast.9, ...), custom_call_target="tpu_custom_call" | custom-call | tf_op jit(solution)/shard_map/pallas_call | solution.py:418
  164.8 5.2 %collective-permute-start = (f32[8,5,128]{2,1,0:T(8,128)}, f32[8,5,128]{2,1,0:T(8,128)S(1)}, u32[]{:S(2)}, u32[]{:S(2)}) collective-permute-start(f32[8,5,128]{2,1,0:T(8,128)} %get-tuple-element.21), channel_id=1, source_target_pairs={{1,0},{2,1},{3,2},{4,3},{5,4},{6,5},{7,6},{8,7},{9,8},{10,9},{11,1... | collective-permute-start | bytes 61448 | tf_op jit(solution)/shard_map/ppermute | solution.py:26
  170.0 1.9 %collective-permute-start.1 = (f32[8,5,128]{2,1,0:T(8,128)}, f32[8,5,128]{2,1,0:T(8,128)S(1)}, u32[]{:S(2)}, u32[]{:S(2)}) collective-permute-start(f32[8,5,128]{2,1,0:T(8,128)} %get-tuple-element.22), channel_id=1, source_target_pairs={{0,1},{1,2},{2,3},{3,4},{4,5},{5,6},{6,7},{7,8},{8,9},{9,10},{10,1... | collective-permute-start | bytes 61448 | tf_op jit(solution)/shard_map/ppermute | solution.py:26
  171.9 0.0 collective-permute-done
  171.9 7.7 %collective-permute-done.1 = f32[8,5,128]{2,1,0:T(8,128)S(1)} collective-permute-done((f32[8,5,128]{2,1,0:T(8,128)}, f32[8,5,128]{2,1,0:T(8,128)S(1)}, u32[]{:S(2)}, u32[]{:S(2)}) %collective-permute-start.1) | collective-permute-done | bytes 20512 | tf_op jit(solution)/shard_map/ppermute | solution.py:26
  179.6 0.6 copy.25
  (2 shorter events, 0.0 us)
Async XLA Ops:
  0.6 15.5 %copy-start.2 = (bf16[8,256,256]{2,1,0:T(8,128)(2,1)S(1)}, bf16[8,256,256]{2,1,0:T(8,128)(2,1)}, u32[]{:S(2)}) copy-start(bf16[8,256,256]{2,1,0:T(8,128)(2,1)} %down_ref.1) | copy-start | bytes 3145732
  2.2 55.0 %copy-start = (f32[256,4,128]{2,1,0:T(4,128)}, f32[256,4,128]{2,1,0:T(4,128)S(1)}, u32[]{:S(2)}) copy-start(f32[256,4,128]{2,1,0:T(4,128)S(1)} %copy.24) | copy-start | bytes 1572868
  10.3 1.2 copy-start.1
  11.6 0.9 copy-start.5
  54.6 1.0 copy-start.3
  55.6 1.0 copy-start.4
  56.6 0.6 copy-start.6
  164.8 7.1 %collective-permute-start = (f32[8,5,128]{2,1,0:T(8,128)}, f32[8,5,128]{2,1,0:T(8,128)S(1)}, u32[]{:S(2)}, u32[]{:S(2)}) collective-permute-start(f32[8,5,128]{2,1,0:T(8,128)} %get-tuple-element.21), channel_id=1, source_target_pairs={{1,0},{2,1},{3,2},{4,3},{5,4},{6,5},{7,6},{8,7},{9,8},{10,9},{11,1... | collective-permute-start | bytes 61448 | tf_op jit(solution)/shard_map/ppermute | solution.py:26
  170.0 9.7 %collective-permute-start.1 = (f32[8,5,128]{2,1,0:T(8,128)}, f32[8,5,128]{2,1,0:T(8,128)S(1)}, u32[]{:S(2)}, u32[]{:S(2)}) collective-permute-start(f32[8,5,128]{2,1,0:T(8,128)} %get-tuple-element.22), channel_id=1, source_target_pairs={{0,1},{1,2},{2,3},{3,4},{4,5},{5,6},{6,7},{7,8},{8,9},{9,10},{10,1... | collective-permute-start | bytes 61448 | tf_op jit(solution)/shard_map/ppermute | solution.py:26

commit v5 on v4

--- a/solution.py
+++ b/solution.py
@@ -17,6 +17,8 @@
 UNROLL = 16
 KSTEP = 8
 WINDOW = 8
+PLACE_STEPS = 65535.0
+CHARGE_STEPS = 32767.0
 SPREAD = 45
 
 
@@ -51,8 +53,22 @@
     lax.fori_loop(0, ref.shape[0] // 16, step, 0, unroll=4)
 
 
+def charge_rows(rows):
+    return lax.rem(lax.broadcasted_iota(jnp.int32, (rows, LANES), 0), 4) == 3
+
+
 def pack_kernel(
-    cell_ids, leaf_ids, own_ref, body_ref, up_ref, out_cells, out_body, share, tab, stage
+    cell_ids,
+    leaf_ids,
+    own_ref,
+    body_ref,
+    up_ref,
+    out_cells,
+    out_body,
+    share,
+    tab,
+    stage,
+    stage_body,
 ):
     ranks, cap, width = out_cells.shape
     blocks = out_body.shape[1] // 4
@@ -64,12 +80,24 @@
             stage[pl.ds(r * 2 * cap + 2 * s, 2), :] = tab[pl.ds(row, 2), :]
         for s in range(blocks):
             row = pl.multiple_of(leaf_ids[r * blocks + s], 4)
-            out_body[r, 4 * s : 4 * s + 4, :] = body_ref[pl.ds(row, 4), :]
+            at = r * 4 * blocks + 4 * s
+            stage_body[pl.ds(at, 4), :] = body_ref[pl.ds(row, 4), :]
         return carry
 
     lax.fori_loop(0, ranks, pick, 0, unroll=2)
 
+    leaves = body_ref.shape[0] // 4
+    biggest = jnp.max(jnp.abs(body_ref[pl.ds(3, leaves, stride=4), :]), axis=0, keepdims=True)
+    biggest = jnp.max(biggest, axis=1, keepdims=True)
+    biggest = jnp.maximum(jnp.broadcast_to(biggest, (1, LANES)), 1e-30)
+    per_unit = CHARGE_STEPS / biggest
+    rows_out = 4 * blocks
+    is_charge = charge_rows(rows_out)
+
     def pack(r, carry):
+        raw = stage_body[pl.ds(pl.multiple_of(r * rows_out, rows_out), rows_out), :]
+        code = jnp.where(is_charge, raw * per_unit + 32768.5, raw * PLACE_STEPS + 0.5)
+        out_body[r] = (code.astype(jnp.int32) - 32768).astype(jnp.int16)
         low = stage[pl.ds(r * 2 * cap, cap, stride=2), :]
         high = stage[pl.ds(r * 2 * cap + 1, cap, stride=2), :]
         out_cells[r] = jnp.concatenate([low, high], 1).astype(BF16)
@@ -91,6 +119,8 @@
     lifted = jnp.sum(lifted, axis=0, keepdims=True)
     share[0:1, :] = lifted[:, :LANES]
     share[1:2, :] = lifted[:, LANES:]
+    share[2:3, :] = biggest
+    share[3:4, :] = jnp.zeros((1, LANES), F32)
 
 
 def pack(cell_ids, leaf_ids, own, body, upward_ops, ranks):
@@ -103,14 +133,15 @@
         pack_kernel,
         out_shape=(
             jax.ShapeDtypeStruct((ranks, cap, width), BF16),
-            jax.ShapeDtypeStruct((ranks, rows, LANES), F32),
-            jax.ShapeDtypeStruct((2, LANES), F32),
+            jax.ShapeDtypeStruct((ranks, rows, LANES), jnp.int16),
+            jax.ShapeDtypeStruct((4, LANES), F32),
         ),
         in_specs=[smem] * 2 + [vmem] * 3,
         out_specs=(vmem,) * 3,
         scratch_shapes=[
             pltpu.VMEM((2 * own.shape[0], LANES), F32),
             pltpu.VMEM((ranks * 2 * cap, LANES), F32),
+            pltpu.VMEM((ranks * rows, LANES), F32),
         ],
         compiler_params=pltpu.CompilerParams(vmem_limit_bytes=32 * 1024 * 1024),
     )(cell_ids, leaf_ids, own, body, upward_ops)
@@ -125,6 +156,7 @@
     got_cells,
     got_body,
     far_ref,
+    scale_ref,
     shares,
     send_sems,
     recv_sems,
@@ -184,12 +216,19 @@
         pair = shares[2 * t] + shares[2 * t + 1]
         return total + weight_ref[top * tops + t] * pair
 
-    coarse = lax.fori_loop(0, tops, weigh, jnp.zeros((2, LANES), F32))
+    coarse = lax.fori_loop(0, tops, weigh, jnp.zeros((4, LANES), F32))
     coarse = jnp.concatenate([coarse[0:1, :], coarse[1:2, :]], 1)
     coarse = jnp.broadcast_to(coarse, (16, width)).astype(BF16)
     for o in range(8):
         out = jnp.dot(coarse, down_ref[o], preferred_element_type=F32)
         far_ref[o : o + 1, :] = out[0:1, :]
+
+
+    def keep_scale(r, carry):
+        scale_ref[pl.ds(r, 1), :] = shares[r, 2:3, :]
+        return carry
+
+    lax.fori_loop(0, ranks, keep_scale, 0)
 
     for copy in keep:
         copy.wait()
@@ -207,13 +246,14 @@
         exchange_kernel,
         out_shape=(
             jax.ShapeDtypeStruct(out_cells.shape, BF16),
-            jax.ShapeDtypeStruct(out_body.shape, F32),
+            jax.ShapeDtypeStruct(out_body.shape, jnp.int16),
             jax.ShapeDtypeStruct((8, width), F32),
+            jax.ShapeDtypeStruct((ranks, LANES), F32),
         ),
         in_specs=[smem, vmem, vmem, hbm, hbm],
-        out_specs=(hbm, hbm, vmem),
+        out_specs=(hbm, hbm, vmem, vmem),
         scratch_shapes=[
-            pltpu.VMEM((ranks, 2, LANES), F32),
+            pltpu.VMEM((ranks, 4, LANES), F32),
             pltpu.SemaphoreType.DMA((3,)),
             pltpu.SemaphoreType.DMA((3,)),
             pltpu.SemaphoreType.DMA((2,)),
@@ -233,7 +273,8 @@
     own_ref,
     got_ref,
     ownp_ref,
-    gotp_ref,
+    coded_ref,
+    scale_ref,
     far_ref,
     moves_ref,
     tr_hbm,
@@ -252,6 +293,7 @@
     window_b,
     near_ref,
     sems,
+    gotp_ref,
     *picked,
     list_width,
     op_count,
@@ -313,6 +355,19 @@
             return carry
 
         lax.fori_loop(0, count, step, 0, unroll=8)
+
+    rank_rows = coded_ref.shape[0] // scale_ref.shape[0]
+    is_charge = charge_rows(rank_rows)
+
+    def decode(r, carry):
+        at = pl.ds(pl.multiple_of(r * rank_rows, rank_rows), rank_rows)
+        code = coded_ref[at, :].astype(jnp.int32).astype(F32)
+        unit = scale_ref[pl.ds(r, 1), :] * (1.0 / CHARGE_STEPS)
+        place = (code + 32768.0) * (1.0 / PLACE_STEPS)
+        gotp_ref[at, :] = jnp.where(is_charge, code * unit, place)
+        return carry
+
+    lax.fori_loop(0, scale_ref.shape[0], decode, 0, unroll=4)
 
     features(ownp_ref, 0, group_lo, True)
     packed(group_lo, target, 0, cells)
@@ -407,7 +462,9 @@
     lax.fori_loop(0, op_count // KSTEP, translate, 0)
 
 
-def main_call(list_width, src, near, ops, own, got, own_p, got_p, far, moves, translate_ops):
+def main_call(
+    list_width, src, near, ops, own, got, own_p, got_p, scale, far, moves, translate_ops
+):
     cells = own.shape[0]
     list_pad = ops.shape[1]
     op_count = translate_ops.shape[0]
@@ -425,7 +482,7 @@
             jax.ShapeDtypeStruct((MCAP, 5, LANES), F32),
             jax.ShapeDtypeStruct((MCAP, 5, LANES), F32),
         ),
-        in_specs=[hbm, hbm] + [vmem] * 6 + [pl.BlockSpec(memory_space=pltpu.SMEM), hbm],
+        in_specs=[hbm, hbm] + [vmem] * 7 + [pl.BlockSpec(memory_space=pltpu.SMEM), hbm],
         out_specs=(vmem,) * 4,
         scratch_shapes=[
             pltpu.VMEM((2 * (cells + got.shape[0]), LANES), F32),
@@ -439,10 +496,11 @@
             pltpu.SMEM((src.shape[0] * WINDOW // cells,), jnp.int32),
             pltpu.SMEM(near.shape, jnp.int32),
             pltpu.SemaphoreType.DMA((4,)),
+            pltpu.VMEM(got_p.shape, F32),
         ]
         + [pltpu.VMEM((2 * list_pad, LANES), F32)] * UNROLL,
         compiler_params=pltpu.CompilerParams(vmem_limit_bytes=60 * 1024 * 1024),
-    )(src, near, ops, own, got, own_p, got_p, far, moves, translate_ops)
+    )(src, near, ops, own, got, own_p, got_p, scale, far, moves, translate_ops)
 
 
 def per_device(
@@ -474,7 +532,7 @@
         upward_ops,
         ranks,
     )
-    got_cells, got_body, far = exchange(
+    got_cells, got_body, far, scale = exchange(
         top_weight.reshape(-1), share, downward_ops, out_cells, out_body
     )
     list_pad = -(-list_operator.shape[1] // 64) * 64
@@ -495,6 +553,7 @@
         got_cells.reshape(-1, width),
         flat,
         got_body.reshape(-1, leaf_size),
+        scale,
         far,
         move_counts,
         translate_ops,

time: 181 us -> 179 us (0.989)
  Pallas kernels: 150 us -> 147 us
    pallas_call x1, Pallas kernels: 38.4 us -> 35.3 us  [exchange(): pl.pallas_call(exchange_kernel, out_shape=(jax.ShapeDtypeStruct(out_cells...]
    unnamed x19 -> x21, local copies, waits for them, and re-layouts: 8.01 us -> 8.42 us
where the time goes in v5:
time: 179 us; the launch traced here: 178 us
  Pallas kernels  147 us (82%)
  local copies, waits for them, and re-layouts  11.8 us (7%)
  waiting for transfers between devices  7.73 us (4%)
  starting transfers between devices  6.98 us (4%)
  other arithmetic  3.54 us (2%)
    pallas_call x1, Pallas kernels, main_call(): pl.pallas_call(functools.partial(main_kernel, list_width=list_width, op_c...  108 us
    pallas_call x1, Pallas kernels, exchange(): pl.pallas_call(exchange_kernel, out_shape=(jax.ShapeDtypeStruct(out_cells...  35.3 us
    unnamed x21, local copies, waits for them, and re-layouts  8.42 us
    ppermute x2, waiting for transfers between devices, shifted(): return lax.ppermute(x, axis, pairs)  7.73 us
    ppermute x2, starting transfers between devices, shifted(): return lax.ppermute(x, axis, pairs)  6.98 us
    pallas_call x1, Pallas kernels, pack(): pl.pallas_call(pack_kernel, out_shape=(jax.ShapeDtypeStruct((ranks, cap,...  4.01 us
  transfers between devices with their start and end apart: 2, of which 1 were waited for; matrix products, arithmetic and copies ran while one was open for 0% of the time, Pallas kernels for 0%

profile of v5, /device:TPU:8, one launch (start us, length us, event | category | flops | bytes accessed | tf_op | source)
XLA Modules:
  0.0 178.0 jit_solution(4906340914897972381)
XLA Ops:
  0.6 0.0 copy-start.2
  0.6 1.2 pad_maximum_fusion
  1.8 0.3 copy.24
  2.2 0.0 copy-start
  2.2 0.7 broadcast_multiply_fusion.1
  2.9 0.1 copy.22
  3.0 0.1 reshape.37.cell_ids
  3.1 0.7 broadcast_multiply_fusion.2
  3.8 0.1 copy.23
  3.9 0.1 reshape.38.leaf_ids
  4.0 0.8 reshape.36.weight_ref
  4.8 0.9 broadcast_multiply_fusion
  5.8 0.1 copy.19
  5.9 0.2 reshape.33
  6.1 0.7 copy.26
  6.8 1.1 copy.21
  7.9 0.9 copy.20
  8.8 0.8 reshape.35.near_hbm
  9.6 0.7 pad.9.op_ref
  10.3 0.0 copy-start.1
  10.3 1.2 copy-done.1
  11.5 0.0 copy-start.4
  11.5 0.9 copy-done.4
  12.4 4.0 %shard_map.148 = (bf16[128,16,256]{2,1,0:T(8,128)(2,1)S(1)}, s16[128,16,128]{2,1,0:T(8,128)(2,1)S(1)}, f32[4,128]{1,0:T(4,128)S(1)}) custom-call(s32[2048]{0:T(1024)S(1)} %reshape.37.cell_ids, s32[512]{0:T(512)S(1)} %reshape.38.leaf_ids, bf16[256,256]{1,0:T(8,128)(2,1)S(1)} %copy-done.4, f32[1024,128]{1,0:T(8,128)S(1)} %bitcast.7, ...), custom_call_target="tpu_custom_call" | custom-call | tf_op jit(solution)/shard_map/pallas_call | solution.py:132
  16.4 0.0 copy-done.2
  16.5 35.3 %shard_map.149 = (bf16[128,16,256]{2,1,0:T(8,128)(2,1)S(1)}, s16[128,16,128]{2,1,0:T(8,128)(2,1)S(1)}, f32[8,256]{1,0:T(8,128)S(1)}, f32[128,128]{1,0:T(8,128)S(1)}) custom-call(f32[4096]{0:T(1024)S(1)} %reshape.36.weight_ref, f32[4,128]{1,0:T(4,128)S(1)} %get-tuple-element.14.share, bf16[8,256,256]{2,1,0:T(8,128)(2,1)S(1)} %copy-done.2, ...), custom_call_target="tpu_custom_call" | custom-call | tf_op jit(solution)/shard_map/pallas_call | solution.py:245
  51.8 0.0 copy-start.3
  51.8 1.0 copy-done.3
  52.8 0.0 copy-start.5
  52.8 0.8 copy-done.5
  53.6 0.0 copy-start.6
  53.6 0.6 copy-done.6
  54.2 0.0 copy-start.7
  54.2 0.6 copy-done.7
  54.8 0.0 copy-done
  54.8 107.8 %shard_map.150 = (f32[256,256]{1,0:T(8,128)}, f32[256,128]{1,0:T(8,128)}, f32[8,5,128]{2,1,0:T(8,128)}, f32[8,5,128]{2,1,0:T(8,128)}) custom-call(s32[65536]{0:T(1024)} %bitcast.11, s32[6912]{0:T(1024)} %reshape.35.near_hbm, s32[256,192]{1,0:T(8,128)} %pad.9.op_ref, bf16[256,256]{1,0:T(8,128)(2,1)} %own_ref.3, bf16[2048,256]{1,0:T(8,128)(2,1)} %bitcast.9, ...), custom_call_target="tpu_custom_call" | custom-call | tf_op jit(solution)/shard_map/pallas_call | solution.py:475
  162.6 5.1 %collective-permute-start = (f32[8,5,128]{2,1,0:T(8,128)}, f32[8,5,128]{2,1,0:T(8,128)S(1)}, u32[]{:S(2)}, u32[]{:S(2)}) collective-permute-start(f32[8,5,128]{2,1,0:T(8,128)} %get-tuple-element.23), channel_id=1, source_target_pairs={{1,0},{2,1},{3,2},{4,3},{5,4},{6,5},{7,6},{8,7},{9,8},{10,9},{11,1... | collective-permute-start | bytes 61448 | tf_op jit(solution)/shard_map/ppermute | solution.py:28
  167.7 1.9 %collective-permute-start.1 = (f32[8,5,128]{2,1,0:T(8,128)}, f32[8,5,128]{2,1,0:T(8,128)S(1)}, u32[]{:S(2)}, u32[]{:S(2)}) collective-permute-start(f32[8,5,128]{2,1,0:T(8,128)} %get-tuple-element.24), channel_id=1, source_target_pairs={{0,1},{1,2},{2,3},{3,4},{4,5},{5,6},{6,7},{7,8},{8,9},{9,10},{10,1... | collective-permute-start | bytes 61448 | tf_op jit(solution)/shard_map/ppermute | solution.py:28
  169.6 0.0 collective-permute-done
  169.6 7.7 %collective-permute-done.1 = f32[8,5,128]{2,1,0:T(8,128)S(1)} collective-permute-done((f32[8,5,128]{2,1,0:T(8,128)}, f32[8,5,128]{2,1,0:T(8,128)S(1)}, u32[]{:S(2)}, u32[]{:S(2)}) %collective-permute-start.1) | collective-permute-done | bytes 20512 | tf_op jit(solution)/shard_map/ppermute | solution.py:28
  177.4 0.6 copy.25
  (2 shorter events, 0.0 us)
Async XLA Ops:
  0.6 15.8 %copy-start.2 = (bf16[8,256,256]{2,1,0:T(8,128)(2,1)S(1)}, bf16[8,256,256]{2,1,0:T(8,128)(2,1)}, u32[]{:S(2)}) copy-start(bf16[8,256,256]{2,1,0:T(8,128)(2,1)} %down_ref.1) | copy-start | bytes 3145732
  2.2 52.6 %copy-start = (f32[256,4,128]{2,1,0:T(4,128)}, f32[256,4,128]{2,1,0:T(4,128)S(1)}, u32[]{:S(2)}) copy-start(f32[256,4,128]{2,1,0:T(4,128)S(1)} %copy.24) | copy-start | bytes 1572868
  10.3 1.2 copy-start.1
  11.5 0.9 copy-start.4
  51.8 1.0 copy-start.3
  52.8 0.8 copy-start.5
  53.6 0.6 copy-start.6
  54.2 0.6 copy-start.7
  162.6 7.0 %collective-permute-start = (f32[8,5,128]{2,1,0:T(8,128)}, f32[8,5,128]{2,1,0:T(8,128)S(1)}, u32[]{:S(2)}, u32[]{:S(2)}) collective-permute-start(f32[8,5,128]{2,1,0:T(8,128)} %get-tuple-element.23), channel_id=1, source_target_pairs={{1,0},{2,1},{3,2},{4,3},{5,4},{6,5},{7,6},{8,7},{9,8},{10,9},{11,1... | collective-permute-start | bytes 61448 | tf_op jit(solution)/shard_map/ppermute | solution.py:28
  167.7 9.7 %collective-permute-start.1 = (f32[8,5,128]{2,1,0:T(8,128)}, f32[8,5,128]{2,1,0:T(8,128)S(1)}, u32[]{:S(2)}, u32[]{:S(2)}) collective-permute-start(f32[8,5,128]{2,1,0:T(8,128)} %get-tuple-element.24), channel_id=1, source_target_pairs={{0,1},{1,2},{2,3},{3,4},{4,5},{5,6},{6,7},{7,8},{8,9},{9,10},{10,1... | collective-permute-start | bytes 61448 | tf_op jit(solution)/shard_map/ppermute | solution.py:28
